TPU v7x, 768 devices: a whole 4x8x12 slice. The times are simulated.
768 devices in a mesh: grp: 48 (over z, x), dev: 16 (over y, core).
Axes of the slice: x: 4, y: 8, z: 12, core: 2. Of those that a mesh axis runs over, the one named last changes fastest.
Arguments:
- block_states: float32 [6144, 5, 4096], P(('grp', 'dev')), may hold values from -2 to 10.5, as said below
- dest_dev: int32 [6144], P('grp'), may hold values from -1 to 15, as said below
- dest_slot: int32 [6144], P('grp'), may hold values from 0 to 3, as said below
- neighbours: int32 [2, 3072], P(None, 'grp'), may hold values from -1 to 63, as said below
- coarse_map: int32 [16, 192], P('dev'), may hold values from 0 to 191, each once within a row
Outputs:
- advanced: float32 [3072, 5, 4096], P(('grp', 'dev'))
- registers: float32 [768, 5, 256], P(('grp', 'dev'))
Inputs may be any that keep to these rules, and one draw needn't show every extreme that they name: `block_states`: every slot holds a physical state: density 0.5 to 2, each velocity component -1 to 1, pressure 0.3 to 3. `dest_dev`: each pair of a receiving device index and a slot 0 .. 3 of a group gets exactly one patch; a device keeps its own patches or sends at most one patch to each of the next 3 device indices of its group (counted modulo 16) and to no other. `dest_slot`: see dest_dev. Index dev * 4 + slot within the group; neighbours are mutual (neighbours[1, a] = b exactly when neighbours[0, b] = a, within a group), a neighbour's index differs from the patch's own by at most 3, and -1 marks a domain boundary. `coarse_map`: for each device index a permutation: value m names register m // 4 in the group order, quadrant m % 4.
All inputs are finite; a program needn't handle non-finite values.
Results may differ from a plain program's by a relative error of at most 0.0003.
Values sent between devices are 32-bit elements; how exact they have to be, the bound alone decides.
A program may use at most 32 MiB of HBM per device.

v0:
```python
import jax
import jax.numpy as jnp
from jax import lax
from jax.sharding import PartitionSpec as P

SIDE_LENGTH = 16
DEVICE_PATCHES = 4
P_DEV = 8


GAMMA = 1.4
COURANT = 0.2


def passed_along(block, axis, distance):
    devices = range(lax.axis_size(axis))
    route = [((i - distance) % len(devices), i) for i in devices]
    return lax.ppermute(block, axis, route)


def shifted(shard, axis, by):
    size = lax.axis_size(axis)
    pairs = [(i, i + by) for i in range(size) if 0 <= i + by < size]
    return lax.ppermute(shard, axis, pairs)


def split_up(shard, dim, size):
    lengths = shard.shape
    tiles = shard.reshape(*lengths[:dim], size, lengths[dim] // size, *lengths[dim + 1 :])
    return jnp.moveaxis(tiles, dim, 0)


def sum_at_owner(shard, axis, dim):
    size = lax.axis_size(axis)
    tiles = lax.all_to_all(split_up(shard, dim, size), axis, 0, 0, tiled=True)
    return jnp.sum(tiles, axis=0)


def primitives(conserved):
    density = conserved[..., 0, :, :]
    inverse = 1.0 / density
    vel_x = conserved[..., 1, :, :] * inverse
    vel_y = conserved[..., 2, :, :] * inverse
    vel_z = conserved[..., 3, :, :] * inverse
    kinetic = 0.5 * (
        conserved[..., 1, :, :] * vel_x
        + conserved[..., 2, :, :] * vel_y
        + conserved[..., 3, :, :] * vel_z
    )
    pressure = (GAMMA - 1.0) * (conserved[..., 4, :, :] - kinetic)
    return jnp.stack([density, vel_x, vel_y, vel_z, pressure], axis=-3)


def euler_flux(primitive):
    density = primitive[..., 0, :, :]
    vel_x = primitive[..., 1, :, :]
    vel_y = primitive[..., 2, :, :]
    vel_z = primitive[..., 3, :, :]
    pressure = primitive[..., 4, :, :]
    mass_flux = density * vel_x
    energy = pressure / (GAMMA - 1.0) + 0.5 * density * (
        vel_x * vel_x + vel_y * vel_y + vel_z * vel_z
    )
    fluxes = jnp.stack(
        [
            mass_flux,
            mass_flux * vel_x + pressure,
            mass_flux * vel_y,
            mass_flux * vel_z,
            vel_x * (energy + pressure),
        ],
        axis=-3,
    )
    conserved = jnp.stack([density, mass_flux, density * vel_y, density * vel_z, energy], axis=-3)
    speeds = jnp.abs(vel_x) + jnp.sqrt(GAMMA * pressure / density)
    return (fluxes, conserved, speeds)


def advance(block_volumes, lower_ghost, upper_ghost):
    extended = jnp.concatenate([lower_ghost, block_volumes, upper_ghost], axis=-2)
    primitive = primitives(extended)
    below_diff = primitive[..., 1:-1, :] - primitive[..., :-2, :]
    above_diff = primitive[..., 2:, :] - primitive[..., 1:-1, :]
    slopes = (
        0.5
        * (jnp.sign(below_diff) + jnp.sign(above_diff))
        * jnp.minimum(jnp.abs(below_diff), jnp.abs(above_diff))
    )
    centre = primitive[..., 1:-1, :]
    left_state = (centre + 0.5 * slopes)[..., :-1, :]
    right_state = (centre - 0.5 * slopes)[..., 1:, :]
    left_flux, left_cons, left_speed = euler_flux(left_state)
    right_flux, right_cons, right_speed = euler_flux(right_state)
    largest = jnp.maximum(left_speed, right_speed)[..., None, :, :]
    interface = 0.5 * (left_flux + right_flux) - 0.5 * largest * (right_cons - left_cons)
    updated = block_volumes - COURANT * (interface[..., 1:, :] - interface[..., :-1, :])
    return (updated, interface[..., -1, :])


def fill_edges(block_volumes, lower_ghost, upper_ghost, lower_nbr, upper_nbr):
    first = block_volumes[:, :, :1, :]
    last = block_volumes[:, :, -1:, :]
    lower_ghost = jnp.where(
        (lower_nbr < 0)[:, None, None, None], jnp.concatenate([first, first], axis=2), lower_ghost
    )
    upper_ghost = jnp.where(
        (upper_nbr < 0)[:, None, None, None], jnp.concatenate([last, last], axis=2), upper_ghost
    )
    return (lower_ghost, upper_ghost)


def coarsen(interface):
    half_edge = SIDE_LENGTH // 2
    shaped = interface.reshape(interface.shape[:-1] + (half_edge, 2, half_edge, 2))
    return shaped.mean(axis=(-3, -1))


def spread(coarse, quadrant):
    half_edge = SIDE_LENGTH // 2
    tiled = jnp.tile(coarse, (1,) * (coarse.ndim - 2) + (2, 2))
    row_ids = jnp.arange(SIDE_LENGTH, dtype=jnp.int32) // half_edge
    inside = (row_ids[:, None] == (quadrant // 2)[..., None, None]) & (
        row_ids[None, :] == (quadrant % 2)[..., None, None]
    )
    placed = tiled * inside.astype(tiled.dtype)[..., None, :, :]
    return placed.reshape(placed.shape[:-2] + (SIDE_LENGTH * SIDE_LENGTH,))


def selected_lines(weights, operand):
    flat = operand.reshape(operand.shape[0], -1)
    picked = jnp.dot(weights, flat, precision=lax.Precision.HIGHEST)
    return picked.reshape((weights.shape[0],) + operand.shape[1:])


def add_faces(totals, arrived, labels, lower_nbr, upper_nbr):
    below_sel = (lower_nbr[:, None] == labels[None, :]).astype(jnp.float32)
    above_sel = (upper_nbr[:, None] == labels[None, :]).astype(jnp.float32)
    return (
        totals[0] + selected_lines(below_sel, arrived[0]),
        totals[1] + selected_lines(above_sel, arrived[1]),
    )


def landing_rows(plan_dev, plan_slot, source_dev, my_dev, wanted):
    from_dev = lax.dynamic_index_in_dim(plan_dev, source_dev, 0, keepdims=False)
    from_slot = lax.dynamic_index_in_dim(plan_slot, source_dev, 0, keepdims=False)
    hits = (from_dev[None, :] == my_dev) & (from_slot[None, :] == wanted[:, None])
    return jnp.any(hits, axis=1).astype(jnp.float32)[:, None]


def local(block_states, dest_dev, dest_slot, neighbours, coarse_map):
    n_dev = lax.axis_size("dev")
    my_dev = lax.axis_index("dev")
    group_me = lax.axis_index("grp")
    cell_fields = block_states.shape[1]
    plane_cell_count = SIDE_LENGTH * SIDE_LENGTH
    wanted = jnp.arange(DEVICE_PATCHES, dtype=jnp.int32)
    mine_dev = lax.dynamic_slice_in_dim(dest_dev, my_dev * P_DEV, P_DEV)
    mine_slot = lax.dynamic_slice_in_dim(dest_slot, my_dev * P_DEV, P_DEV)
    retained_lines = (
        (mine_dev[None, :] == my_dev) & (mine_slot[None, :] == wanted[:, None])
    ).astype(jnp.float32)
    plan_dev = dest_dev.reshape(n_dev, P_DEV)
    plan_slot = dest_slot.reshape(n_dev, P_DEV)
    lower_all = neighbours[0]
    upper_all = neighbours[1]
    redistributed_blocks = selected_lines(retained_lines, block_states)
    for distance in range(1, DEVICE_PATCHES):
        target_dev = (my_dev + distance) % n_dev
        source_dev = (my_dev + n_dev - distance) % n_dev
        sending = (mine_dev == target_dev).astype(jnp.float32)[None, :]
        arrived = passed_along(selected_lines(sending, block_states), "dev", distance)
        redistributed_blocks = redistributed_blocks + selected_lines(
            landing_rows(plan_dev, plan_slot, source_dev, my_dev, wanted), arrived
        )
    block_volumes = redistributed_blocks.reshape(
        DEVICE_PATCHES, cell_fields, SIDE_LENGTH, plane_cell_count
    )
    lower_nbr = lax.dynamic_slice_in_dim(lower_all, my_dev * DEVICE_PATCHES, DEVICE_PATCHES)
    upper_nbr = lax.dynamic_slice_in_dim(upper_all, my_dev * DEVICE_PATCHES, DEVICE_PATCHES)
    top_layers = block_volumes[:, :, SIDE_LENGTH - 2 :, :]
    bottom_layers = block_volumes[:, :, :2, :]
    empty = jnp.zeros((DEVICE_PATCHES, cell_fields, 2, plane_cell_count), jnp.float32)
    ghosts = add_faces(
        (empty, empty),
        (top_layers, bottom_layers),
        my_dev * DEVICE_PATCHES + wanted,
        lower_nbr,
        upper_nbr,
    )
    from_below = shifted((top_layers, bottom_layers), "dev", 1)
    labels_below = jnp.where(my_dev > 0, (my_dev - 1) * DEVICE_PATCHES + wanted, -3)
    ghosts = add_faces(ghosts, from_below, labels_below, lower_nbr, upper_nbr)
    from_above = shifted((top_layers, bottom_layers), "dev", -1)
    labels_above = jnp.where(my_dev < n_dev - 1, (my_dev + 1) * DEVICE_PATCHES + wanted, -3)
    ghosts = add_faces(ghosts, from_above, labels_above, lower_nbr, upper_nbr)
    lower_ghost, upper_ghost = ghosts
    lower_ghost, upper_ghost = fill_edges(
        block_volumes, lower_ghost, upper_ghost, lower_nbr, upper_nbr
    )
    advanced, interface = advance(block_volumes, lower_ghost, upper_ghost)
    out_state = advanced.reshape(DEVICE_PATCHES, cell_fields, SIDE_LENGTH**3)
    column = coarse_map[0]
    targets = lax.dynamic_slice_in_dim(column, group_me * DEVICE_PATCHES, DEVICE_PATCHES)
    placed = spread(coarsen(interface), targets % DEVICE_PATCHES)
    row_ids = jnp.arange(1 * lax.axis_size("grp"), dtype=jnp.int32)
    chosen = ((targets // DEVICE_PATCHES)[None, :] == row_ids[:, None]).astype(jnp.float32)
    registers = sum_at_owner(selected_lines(chosen, placed), "grp", 0)
    return (out_state, registers)


def solution(mesh):
    in_specs = (P(("grp", "dev"), None, None), P("grp"), P("grp"), P(None, "grp"), P("dev", None))
    out_specs = (P(("grp", "dev"), None, None), P(("grp", "dev"), None, None))
    return jax.shard_map(local, mesh=mesh, in_specs=in_specs, out_specs=out_specs, check_vma=False)
```

profile of v0, /device:TPU:25, one launch (start us, length us, event | category | flops | bytes accessed | tf_op | source)
XLA Modules:
  0.0 74.6 jit_solution(2075148908092296457)
XLA Ops:
  0.7 0.7 copy-done.1
  1.5 0.3 copy-done
  1.7 0.4 fusion.2
  2.2 5.1 %collective-permute-start.2 = (f32[1,5,4096]{2,1,0:T(8,128)S(1)}, f32[1,5,4096]{2,1,0:T(8,128)S(1)}, u32[]{:S(2)}, u32[]{:S(2)}) collective-permute-start(f32[1,5,4096]{2,1,0:T(8,128)S(1)} %copy.67), channel_id=1, source_target_pairs={{13,0},{14,1},{15,2},{0,3},{1,4},{2,5},{3,6},{4,7},{5,8},{6,9},{7,... | collective-permute-start | bytes 245768 | tf_op jit(solution)/shard_map/ppermute | solution.py:18
  7.3 0.4 fusion.4
  7.8 2.3 %collective-permute-start.1 = (f32[1,5,4096]{2,1,0:T(8,128)S(1)}, f32[1,5,4096]{2,1,0:T(8,128)S(1)}, u32[]{:S(2)}, u32[]{:S(2)}) collective-permute-start(f32[1,5,4096]{2,1,0:T(8,128)S(1)} %copy.66), channel_id=1, source_target_pairs={{14,0},{15,1},{0,2},{1,3},{2,4},{3,5},{4,6},{5,7},{6,8},{7,9},{8,1... | collective-permute-start | bytes 245768 | tf_op jit(solution)/shard_map/ppermute | solution.py:18
  10.1 0.4 fusion.6
  10.6 0.3 collective-permute-start
  11.0 0.6 copy-done.3
  11.7 0.7 copy-done.4
  13.0 0.7 copy-done.2
  14.1 0.9 %collective-permute-done.1 = f32[1,5,4096]{2,1,0:T(8,128)S(1)} collective-permute-done((f32[1,5,4096]{2,1,0:T(8,128)S(1)}, f32[1,5,4096]{2,1,0:T(8,128)S(1)}, u32[]{:S(2)}, u32[]{:S(2)}) %collective-permute-start.1) | collective-permute-done | bytes 81952 | tf_op jit(solution)/shard_map/ppermute | solution.py:18
  15.0 1.1 %collective-permute-done = f32[1,5,4096]{2,1,0:T(8,128)S(1)} collective-permute-done((f32[1,5,4096]{2,1,0:T(8,128)S(1)}, f32[1,5,4096]{2,1,0:T(8,128)S(1)}, u32[]{:S(2)}, u32[]{:S(2)}) %collective-permute-start) | collective-permute-done | bytes 81952 | tf_op jit(solution)/shard_map/ppermute | solution.py:18
  16.1 0.5 multiply_add_fusion
  16.6 0.2 reshape.302
  17.0 5.6 %collective-permute-start.5 = (f32[4,5,2,256]{3,2,1,0:T(2,128)S(1)}, f32[4,5,2,256]{3,2,1,0:T(2,128)S(1)}, u32[]{:S(2)}, u32[]{:S(2)}) collective-permute-start(f32[4,5,2,256]{3,2,1,0:T(2,128)S(1)} %copy.75), channel_id=1, source_target_pairs={{0,1},{1,2},{2,3},{3,4},{4,5},{5,6},{6,7},{7,8},{8,9},{9,10},{10,1... | collective-permute-start | bytes 122888 | tf_op jit(solution)/shard_map/ppermute | solution.py:24
  22.6 1.9 %collective-permute-start.6 = (f32[4,5,2,256]{3,2,1,0:T(2,128)S(1)}, f32[4,5,2,256]{3,2,1,0:T(2,128)S(1)}, u32[]{:S(2)}, u32[]{:S(2)}) collective-permute-start(f32[4,5,2,256]{3,2,1,0:T(2,128)S(1)} %copy.75), channel_id=1, source_target_pairs={{1,0},{2,1},{3,2},{4,3},{5,4},{6,5},{7,6},{8,7},{9,8},{10,9},{11,1... | collective-permute-start | bytes 122888 | tf_op jit(solution)/shard_map/ppermute | solution.py:24
  24.6 4.9 %collective-permute-start.3 = (f32[4,5,2,256]{3,2,1,0:T(2,128)S(1)}, f32[4,5,2,256]{3,2,1,0:T(2,128)S(1)}, u32[]{:S(2)}, u32[]{:S(2)}) collective-permute-start(f32[4,5,2,256]{3,2,1,0:T(2,128)S(1)} %copy.74), channel_id=1, source_target_pairs={{0,1},{1,2},{2,3},{3,4},{4,5},{5,6},{6,7},{7,8},{8,9},{9,10},{10,1... | collective-permute-start | bytes 122888 | tf_op jit(solution)/shard_map/ppermute | solution.py:24
  29.4 1.9 %collective-permute-start.4 = (f32[4,5,2,256]{3,2,1,0:T(2,128)S(1)}, f32[4,5,2,256]{3,2,1,0:T(2,128)S(1)}, u32[]{:S(2)}, u32[]{:S(2)}) collective-permute-start(f32[4,5,2,256]{3,2,1,0:T(2,128)S(1)} %copy.74), channel_id=1, source_target_pairs={{1,0},{2,1},{3,2},{4,3},{5,4},{6,5},{7,6},{8,7},{9,8},{10,9},{11,1... | collective-permute-start | bytes 122888 | tf_op jit(solution)/shard_map/ppermute | solution.py:24
  32.2 0.2 fusion
  32.7 3.2 %collective-permute-done.4 = f32[4,5,2,256]{3,2,1,0:T(2,128)S(1)} collective-permute-done((f32[4,5,2,256]{3,2,1,0:T(2,128)S(1)}, f32[4,5,2,256]{3,2,1,0:T(2,128)S(1)}, u32[]{:S(2)}, u32[]{:S(2)}) %collective-permute-start.4) | collective-permute-done | bytes 40992 | tf_op jit(solution)/shard_map/ppermute | solution.py:24
  36.0 0.2 fusion.1
  36.6 0.4 slice_add_fusion
  38.3 0.4 reduce_sum.20
  38.7 0.3 copy.63
  39.1 0.5 tile.10
  39.6 0.4 convolution_bitcast_fusion
  40.0 0.9 %copy.64 = f32[48,1,5,256]{3,1,2,0:T(1,128)} copy(f32[48,1,5,256]{3,0,2,1:T(8,128)S(1)} %convolution_bitcast_fusion) | data formatting | bytes 491520 | tf_op jit(solution)/shard_map/dot_general | solution.py:131
  40.9 18.0 %all-to-all-start = ((f32[48,1,5,256]{3,1,2,0:T(1,128)}), f32[48,1,5,256]{3,1,2,0:T(1,128)S(1)}, u32[]{:S(2)}, u32[]{:S(2)}) async-start(f32[48,1,5,256]{3,1,2,0:T(1,128)} %copy.64), calls=%async_computation | async-start | bytes 491520 | tf_op jit(solution)/shard_map/all_to_all | solution.py:35
  58.9 0.8 %fusion.11 = f32[4,5,16,256]{3,0,2,1:T(4,128)} fusion(f32[4,5,16,256]{3,0,2,1:T(4,128)S(1)} %bitcast.135, f32[4,5,17,256]{3,0,2,1:T(4,128)S(1)} %multiply_subtract_fusion), kind=kLoop, calls=%fused_computation.22 | loop fusion | flops 245760 | bytes 1310720 | tf_op jit(solution)/shard_map/sub | solution.py:96
  59.8 14.1 %all-to-all-done = f32[48,1,5,256]{3,1,2,0:T(1,128)S(1)} async-done(((f32[48,1,5,256]{3,1,2,0:T(1,128)}), f32[48,1,5,256]{3,1,2,0:T(1,128)S(1)}, u32[]{:S(2)}, u32[]{:S(2)}) %all-to-all-start) | async-done | bytes 245792 | tf_op jit(solution)/shard_map/all_to_all | solution.py:35
  74.0 0.6 reduce_sum.22
  (80 shorter events, 4.5 us)
Async XLA Ops:
  0.6 1.1 %copy-start = (f32[8,5,4096]{2,0,1:T(8,128)S(1)}, f32[8,5,4096]{2,0,1:T(8,128)}, u32[]{:S(2)}) copy-start(f32[8,5,4096]{2,0,1:T(8,128)} %param.5) | copy-start | bytes 1966084
  0.7 0.7 copy-start.1
  2.2 11.9 %collective-permute-start.2 = (f32[1,5,4096]{2,1,0:T(8,128)S(1)}, f32[1,5,4096]{2,1,0:T(8,128)S(1)}, u32[]{:S(2)}, u32[]{:S(2)}) collective-permute-start(f32[1,5,4096]{2,1,0:T(8,128)S(1)} %copy.67), channel_id=1, source_target_pairs={{13,0},{14,1},{15,2},{0,3},{1,4},{2,5},{3,6},{4,7},{5,8},{6,9},{7,... | collective-permute-start | bytes 245768 | tf_op jit(solution)/shard_map/ppermute | solution.py:18
  7.8 7.2 %collective-permute-start.1 = (f32[1,5,4096]{2,1,0:T(8,128)S(1)}, f32[1,5,4096]{2,1,0:T(8,128)S(1)}, u32[]{:S(2)}, u32[]{:S(2)}) collective-permute-start(f32[1,5,4096]{2,1,0:T(8,128)S(1)} %copy.66), channel_id=1, source_target_pairs={{14,0},{15,1},{0,2},{1,3},{2,4},{3,5},{4,6},{5,7},{6,8},{7,9},{8,1... | collective-permute-start | bytes 245768 | tf_op jit(solution)/shard_map/ppermute | solution.py:18
  10.6 5.5 %collective-permute-start = (f32[1,5,4096]{2,1,0:T(8,128)S(1)}, f32[1,5,4096]{2,1,0:T(8,128)S(1)}, u32[]{:S(2)}, u32[]{:S(2)}) collective-permute-start(f32[1,5,4096]{2,1,0:T(8,128)S(1)} %copy.65), channel_id=1, source_target_pairs={{15,0},{0,1},{1,2},{2,3},{3,4},{4,5},{5,6},{6,7},{7,8},{8,9},{9,10... | collective-permute-start | bytes 245768 | tf_op jit(solution)/shard_map/ppermute | solution.py:18
  10.9 0.7 copy-start.3
  11.7 0.7 copy-start.4
  12.9 0.7 copy-start.2
  17.0 14.9 %collective-permute-start.5 = (f32[4,5,2,256]{3,2,1,0:T(2,128)S(1)}, f32[4,5,2,256]{3,2,1,0:T(2,128)S(1)}, u32[]{:S(2)}, u32[]{:S(2)}) collective-permute-start(f32[4,5,2,256]{3,2,1,0:T(2,128)S(1)} %copy.75), channel_id=1, source_target_pairs={{0,1},{1,2},{2,3},{3,4},{4,5},{5,6},{6,7},{7,8},{8,9},{9,10},{10,1... | collective-permute-start | bytes 122888 | tf_op jit(solution)/shard_map/ppermute | solution.py:24
  22.6 9.6 %collective-permute-start.6 = (f32[4,5,2,256]{3,2,1,0:T(2,128)S(1)}, f32[4,5,2,256]{3,2,1,0:T(2,128)S(1)}, u32[]{:S(2)}, u32[]{:S(2)}) collective-permute-start(f32[4,5,2,256]{3,2,1,0:T(2,128)S(1)} %copy.75), channel_id=1, source_target_pairs={{1,0},{2,1},{3,2},{4,3},{5,4},{6,5},{7,6},{8,7},{9,8},{10,9},{11,1... | collective-permute-start | bytes 122888 | tf_op jit(solution)/shard_map/ppermute | solution.py:24
  24.6 7.9 %collective-permute-start.3 = (f32[4,5,2,256]{3,2,1,0:T(2,128)S(1)}, f32[4,5,2,256]{3,2,1,0:T(2,128)S(1)}, u32[]{:S(2)}, u32[]{:S(2)}) collective-permute-start(f32[4,5,2,256]{3,2,1,0:T(2,128)S(1)} %copy.74), channel_id=1, source_target_pairs={{0,1},{1,2},{2,3},{3,4},{4,5},{5,6},{6,7},{7,8},{8,9},{9,10},{10,1... | collective-permute-start | bytes 122888 | tf_op jit(solution)/shard_map/ppermute | solution.py:24
  29.4 6.5 %collective-permute-start.4 = (f32[4,5,2,256]{3,2,1,0:T(2,128)S(1)}, f32[4,5,2,256]{3,2,1,0:T(2,128)S(1)}, u32[]{:S(2)}, u32[]{:S(2)}) collective-permute-start(f32[4,5,2,256]{3,2,1,0:T(2,128)S(1)} %copy.74), channel_id=1, source_target_pairs={{1,0},{2,1},{3,2},{4,3},{5,4},{6,5},{7,6},{8,7},{9,8},{10,9},{11,1... | collective-permute-start | bytes 122888 | tf_op jit(solution)/shard_map/ppermute | solution.py:24
  40.9 32.9 %all-to-all-start = ((f32[48,1,5,256]{3,1,2,0:T(1,128)}), f32[48,1,5,256]{3,1,2,0:T(1,128)S(1)}, u32[]{:S(2)}, u32[]{:S(2)}) async-start(f32[48,1,5,256]{3,1,2,0:T(1,128)} %copy.64), calls=%async_computation | async-start | bytes 491520 | tf_op jit(solution)/shard_map/all_to_all | solution.py:35
where the time goes:
time: 75 us; the launch traced here: 74.6 us
  starting transfers between devices  40 us (53%)
  waiting for transfers between devices  19.3 us (26%)
  local copies, waits for them, and re-layouts  6.68 us (9%)
  other arithmetic  3.97 us (5%)
  matrix products  3.47 us (5%)
  between operations  1.16 us (2%)
    all_to_all x1, starting transfers between devices, sum_at_owner(): tiles = lax.all_to_all(split_up(shard, dim, size), axis, 0, 0, tiled=True)  18 us
    ppermute x4, starting transfers between devices, shifted(): return lax.ppermute(shard, axis, pairs)  14.3 us
    all_to_all x1, waiting for transfers between devices, sum_at_owner(): tiles = lax.all_to_all(split_up(shard, dim, size), axis, 0, 0, tiled=True)  14.1 us
    ppermute x3, starting transfers between devices, passed_along(): return lax.ppermute(block, axis, route)  7.69 us
    dot_general x11, matrix products, selected_lines(): picked = jnp.dot(weights, flat, precision=lax.Precision.HIGHEST)  3.47 us
    ppermute x4, waiting for transfers between devices, shifted(): return lax.ppermute(shard, axis, pairs)  3.25 us
    unnamed x15, local copies, waits for them, and re-layouts  2.99 us
    ppermute x3, waiting for transfers between devices, passed_along(): return lax.ppermute(block, axis, route)  2.02 us
  transfers between devices with their start and end apart: 8, of which 4 were waited for; matrix products, arithmetic and copies ran while one was open for 6% of the time, Pallas kernels for 0%

commit v1 on v0

v1 whole, which is shorter than its diff:
```python
import functools

import jax
import jax.numpy as jnp
from jax import lax
from jax.experimental import pallas as pl
from jax.experimental.pallas import tpu as pltpu
from jax.sharding import PartitionSpec as P

X_CHIPS = 4
FIELDS = 5
PATCHES = 4
SLOTS = 8
GAMMA = 1.4
COURANT = 0.2
MESH = pl.DeviceIdType.MESH
HIGHEST = lax.Precision.HIGHEST
HOPS = 3

FACE = 40
INNER = 120


def primitives(u):
    inverse = 1.0 / u[0]
    vx, vy, vz = u[1] * inverse, u[2] * inverse, u[3] * inverse
    kinetic = 0.5 * (u[1] * vx + u[2] * vy + u[3] * vz)
    return [u[0], vx, vy, vz, (GAMMA - 1.0) * (u[4] - kinetic)]


def half_slopes(below, centre, above):
    out = []
    for b, c, a in zip(below, centre, above):
        down, up = c - b, a - c
        slope = jnp.maximum(0.0, jnp.minimum(down, up)) + jnp.minimum(0.0, jnp.maximum(down, up))
        out.append(0.5 * slope)
    return out


def euler_flux(prim):
    r, vx, vy, vz, p = prim
    mass = r * vx
    energy = p * (1.0 / (GAMMA - 1.0)) + 0.5 * r * (vx * vx + vy * vy + vz * vz)
    flux = [mass, mass * vx + p, mass * vy, mass * vz, vx * (energy + p)]
    cons = [r, mass, r * vy, r * vz, energy]
    return flux, cons, jnp.abs(vx) + jnp.sqrt(GAMMA * p / r)


def interface(left_prim, left_half, right_prim, right_half):
    left = [c + s for c, s in zip(left_prim, left_half)]
    right = [c - s for c, s in zip(right_prim, right_half)]
    lf, lc, ls = euler_flux(left)
    rf, rc, rs = euler_flux(right)
    largest = 0.5 * jnp.maximum(ls, rs)
    return [0.5 * (a + b) - largest * (d - c) for a, b, c, d in zip(lf, rf, lc, rc)]


def iota(shape, dim):
    return lax.broadcasted_iota(jnp.int32, shape, dim)


def kernel(
    nz, nx, n_dev,
    blk, ddev, dslot, nbr, cmap,
    adv, reg,
    slot_face, slot_inner, face_send, face_recv, inner_send, inner_recv, near, outer, lower, upper, inner,
    xpool, zbuf, zrecv, adv_buf,
    face_ss, face_rs, inner_ss, inner_rs, ghost_ss, ghost_rs, x_ss, x_rs, z_ss, z_rs, out_sem,
):
    me = lax.axis_index("dev")
    grp = lax.axis_index("grp")
    mz, mx = grp // nx, grp % nx
    dev_at = lambda by: {"dev": lax.rem(me + by + n_dev, n_dev)}
    x_at = lambda by: {"grp": mz * nx + lax.rem(mx + by, nx)}
    z_at = lambda by: {"grp": lax.rem(mz + by, nz) * nx + mx}

    barrier = pltpu.get_barrier_semaphore()
    for by in (-1, -2, -3, 1):
        pl.semaphore_signal(barrier, inc=1, device_id=dev_at(by), device_id_type=MESH)
    for by in range(1, nx):
        pl.semaphore_signal(barrier, inc=1, device_id=x_at(by), device_id_type=MESH)
    for by in range(1, nz):
        pl.semaphore_signal(barrier, inc=1, device_id=z_at(by), device_id_type=MESH)

    for j in range(SLOTS):
        for f in range(FIELDS):
            for part, first in ((0, 0), (4, 28)):
                slot_face[j, pl.ds(f * 8 + part, 4), :] = blk[
                    pl.ds((f * 32 + first) * SLOTS + j, 4, stride=SLOTS), :]

    going = []
    for k in range(1, HOPS + 1):
        target = lax.rem(me + k, n_dev)
        slot = jnp.int32(0)
        for j in range(SLOTS):
            slot = jnp.where(ddev[me * SLOTS + j] == target, j, slot)
        going.append(slot)
    for k in range(HOPS):
        face_send[k] = slot_face[going[k]]

    pl.semaphore_wait(barrier, 4 + (nx - 1) + (nz - 1))

    face_copies = []
    for k in range(HOPS):
        copy = pltpu.make_async_remote_copy(
            src_ref=face_send.at[k], dst_ref=face_recv.at[k],
            send_sem=face_ss.at[k], recv_sem=face_rs.at[k], device_id=dev_at(k + 1), device_id_type=MESH)
        copy.start()
        face_copies.append(copy)

    own_slot = []
    for q in range(PATCHES):
        slot = jnp.int32(0)
        for j in range(SLOTS):
            i = me * SLOTS + j
            slot = jnp.where((ddev[i] == me) & (dslot[i] == q), j, slot)
        own_slot.append(slot)
    origin = [jnp.int32(0)] * PATCHES
    for k in range(1, HOPS + 1):
        source = lax.rem(me - k + n_dev, n_dev)
        landing = jnp.int32(-1)
        for j in range(SLOTS):
            i = source * SLOTS + j
            landing = jnp.where(ddev[i] == me, dslot[i], landing)
        for q in range(PATCHES):
            origin[q] = jnp.where(landing == q, k, origin[q])

    for j in range(SLOTS):
        for f in range(FIELDS):
            slot_inner[j, pl.ds(f * 24, 24), :] = blk[pl.ds((f * 32 + 4) * SLOTS + j, 24, stride=SLOTS), :]
    for k in range(HOPS):
        inner_send[k] = slot_inner[going[k]]

    lane32 = iota((8, 8 * nx), 1)
    row8 = iota((8, 8 * nx), 0)
    target = jnp.zeros((8, 8 * nx), jnp.int32)
    for i in range(nx):
        source = mz * nx + lax.rem(mx - i + nx, nx)
        for q in range(PATCHES):
            at = (lane32 >> 3 == i) & ((lane32 & 3) == q)
            target = jnp.where(at, cmap[0, source * PATCHES + q], target)
    same_half = (row8 >> 2) == ((lane32 >> 2) & 1)
    route = []
    for i in range(nz):
        code = (lax.rem(mz + i, nz) * nx + mx) * PATCHES
        hit = (target == code + (row8 & 3)) & same_half
        route.append(jnp.where(hit, 1.0, 0.0))
    route = jnp.concatenate(route, axis=0)

    for copy in face_copies:
        copy.wait_recv()
    for q in range(PATCHES):
        arrived = jnp.maximum(origin[q] - 1, 0)
        face = jnp.where(origin[q] > 0, face_recv[arrived], slot_face[own_slot[q]])
        near[PATCHES + q] = face
        outer[pl.ds(q, FACE, stride=PATCHES), :] = face

    ghost_copies = []
    for n, (by, first, to) in enumerate(((1, 1, 1), (-1, 0, 2 * PATCHES))):
        copy = pltpu.make_async_remote_copy(
            src_ref=near.at[pl.ds(PATCHES + first, 3)], dst_ref=near.at[pl.ds(to, 3)],
            send_sem=ghost_ss.at[n], recv_sem=ghost_rs.at[n], device_id=dev_at(by), device_id_type=MESH)
        copy.start()
        ghost_copies.append(copy)
    inner_copies = []
    for k in range(HOPS):
        copy = pltpu.make_async_remote_copy(
            src_ref=inner_send.at[k], dst_ref=inner_recv.at[k],
            send_sem=inner_ss.at[k], recv_sem=inner_rs.at[k], device_id=dev_at(k + 1), device_id_type=MESH)
        copy.start()
        inner_copies.append(copy)

    patch = iota((8, 128), 0) & 3
    lower_nbr = [nbr[0, me * PATCHES + q] for q in range(PATCHES)]
    upper_nbr = [nbr[1, me * PATCHES + q] for q in range(PATCHES)]
    lower_ids = jnp.zeros((8, 128), jnp.int32)
    upper_ids = jnp.zeros((8, 128), jnp.int32)
    for q in range(PATCHES):
        lower_ids = jnp.where(patch == q, lower_nbr[q], lower_ids)
        upper_ids = jnp.where(patch == q, upper_nbr[q], upper_ids)

    def neighbour(nb, q):
        place = jnp.where(nb < 0, PATCHES + q, nb - (me - 1) * PATCHES)
        return near[jnp.minimum(jnp.maximum(place, 0), 3 * PATCHES - 1)]

    for copy in ghost_copies:
        copy.wait_recv()
    for q in range(PATCHES):
        upper[pl.ds(q, FACE, stride=PATCHES), :] = neighbour(upper_nbr[q], q)

    own = lambda side, layer, f: outer[pl.ds(f * 32 + side * 16 + layer * 8, 8), :]
    last = [own(1, 1, f) for f in range(FIELDS)]
    ghosts_above = [
        [jnp.where(upper_ids < 0, last[f], upper[pl.ds(f * 32 + layer * 8, 8), :]) for f in range(FIELDS)]
        for layer in range(2)]
    p14 = primitives([own(1, 0, f) for f in range(FIELDS)])
    p15 = primitives(last)
    p16 = primitives(ghosts_above[0])
    p17 = primitives(ghosts_above[1])
    s15 = half_slopes(p14, p15, p16)
    s16 = half_slopes(p15, p16, p17)
    top_flux = interface(p15, s15, p16, s16)

    lane_in, lane_out = iota((128, 128), 0), iota((128, 128), 1)
    mean = jnp.where(
        (lane_in >> 5 == (lane_out >> 3) & 3) & ((lane_in & 15) >> 1 == (lane_out & 7)), 0.25, 0.0)
    coarse = jnp.dot(jnp.concatenate(top_flux, axis=0), mean, precision=HIGHEST, preferred_element_type=jnp.float32)
    lane8 = iota((8, 128), 1)
    packed = coarse[0:8]
    for f in range(1, 4):
        packed = jnp.where(lane8 >> 5 == f, coarse[f * 8:f * 8 + 8], packed)
    xpool[0:8, :] = packed
    xpool[8:16, :] = coarse[32:40]
    x_copies = []
    for i in range(1, nx):
        copy = pltpu.make_async_remote_copy(
            src_ref=xpool.at[pl.ds(0, 16)], dst_ref=xpool.at[pl.ds(i * 16, 16)],
            send_sem=x_ss.at[i - 1], recv_sem=x_rs.at[i - 1], device_id=x_at(i), device_id_type=MESH)
        copy.start()
        x_copies.append(copy)

    for q in range(PATCHES):
        lower[pl.ds(q, FACE, stride=PATCHES), :] = neighbour(lower_nbr[q], q)

    for copy in x_copies:
        copy.wait_recv()
    for v in range(2):
        pool = jnp.concatenate([xpool[i * 16 + v * 8:i * 16 + v * 8 + 8, :] for i in range(nx)], axis=0)
        routed = jnp.dot(route, pool, precision=HIGHEST, preferred_element_type=jnp.float32)
        for i in range(nz):
            zbuf[i * 16 + v * 8:i * 16 + v * 8 + 8, :] = routed[i * 8:i * 8 + 8]
    z_copies = []
    for i in range(1, nz):
        copy = pltpu.make_async_remote_copy(
            src_ref=zbuf.at[pl.ds(i * 16, 16)], dst_ref=zrecv.at[pl.ds((i - 1) * 16, 16)],
            send_sem=z_ss.at[i - 1], recv_sem=z_rs.at[i - 1], device_id=z_at(i), device_id_type=MESH)
        copy.start()
        z_copies.append(copy)

    for copy in inner_copies:
        copy.wait_recv()
    for q in range(PATCHES):
        arrived = jnp.maximum(origin[q] - 1, 0)
        for f in range(FIELDS):
            mine = slot_inner[own_slot[q], pl.ds(f * 24, 24), :]
            theirs = inner_recv[arrived, pl.ds(f * 24, 24), :]
            inner[pl.ds(f * 96 + q, 24, stride=PATCHES), :] = jnp.where(origin[q] > 0, theirs, mine)

    first = [own(0, 0, f) for f in range(FIELDS)]
    ghosts_below = [
        [jnp.where(lower_ids < 0, first[f], lower[pl.ds(f * 32 + 16 + layer * 8, 8), :]) for f in range(FIELDS)]
        for layer in range(2)]

    def layer(x):
        if x < 2:
            return [own(0, x, f) for f in range(FIELDS)]
        if x >= 14:
            return [own(1, x - 14, f) for f in range(FIELDS)]
        return [inner[pl.ds(f * 96 + (x - 2) * 8, 8), :] for f in range(FIELDS)]

    here, above = primitives(ghosts_below[1]), primitives(first)
    slope = half_slopes(primitives(ghosts_below[0]), here, above)
    below_flux = None
    for x in range(17):
        beyond = p17 if x == 16 else p16 if x == 15 else primitives(layer(x + 1))
        slope_above = half_slopes(here, above, beyond)
        flux = top_flux if x == 16 else interface(here, slope, above, slope_above)
        if x > 0:
            u = layer(x - 1)
            for f in range(FIELDS):
                adv_buf[pl.ds(f * 128 + (x - 1) * 8, 8), :] = u[f] - COURANT * (flux[f] - below_flux[f])
        here, above, slope, below_flux = above, beyond, slope_above, flux
    out = pltpu.make_async_copy(adv_buf, adv, out_sem)
    out.start()

    for copy in z_copies:
        copy.wait_recv()
    totals = []
    for v in range(2):
        total = zbuf[v * 8:v * 8 + 8, :]
        for i in range(nz - 1):
            total = total + zrecv[i * 16 + v * 8:i * 16 + v * 8 + 8, :]
        totals.append(total)
    parts = [jnp.where(lane8 >> 5 == f, totals[0], 0.0) for f in range(4)]
    parts.append(jnp.where(lane8 >> 5 == 0, totals[1], 0.0))
    place = jnp.where(
        (lane_in & 31) == ((lane_out >> 4) & 3) * 8 + (lane_out & 7), 1.0, 0.0)
    wide = jnp.dot(jnp.concatenate(parts, axis=0), place, precision=HIGHEST, preferred_element_type=jnp.float32)
    row = iota((8, 128), 0)
    inside = (row >> 2 == lane8 >> 6) & ((row & 1) == ((lane8 >> 3) & 1))
    for f in range(FIELDS):
        block = wide[f * 8:f * 8 + 8]
        for half in range(2):
            chosen = jnp.where(inside & ((row & 3) >> 1 == half), block, 0.0)
            reg[pl.ds(f * 2 + half, 1), :] = jnp.sum(chosen, axis=0, keepdims=True)

    for copy in face_copies + ghost_copies + inner_copies + x_copies + z_copies:
        copy.wait_send()
    out.wait()


def solution(mesh):
    n_grp, n_dev = mesh.shape["grp"], mesh.shape["dev"]
    nx = X_CHIPS
    nz = n_grp // nx

    def local(block_states, dest_dev, dest_slot, neighbours, coarse_map):
        blocks = block_states.reshape(SLOTS, FIELDS, 32, 128).transpose(1, 2, 0, 3).reshape(FIELDS * 32 * SLOTS, 128)
        vmem = pl.BlockSpec(memory_space=pltpu.VMEM)
        smem = pl.BlockSpec(memory_space=pltpu.SMEM)
        f32 = jnp.float32
        dma = lambda n: pltpu.SemaphoreType.DMA((n,))
        advanced, registers = pl.pallas_call(
            functools.partial(kernel, nz, nx, n_dev),
            out_shape=(jax.ShapeDtypeStruct((640, 128), f32), jax.ShapeDtypeStruct((10, 128), f32)),
            in_specs=[vmem, smem, smem, smem, smem],
            out_specs=(pl.BlockSpec(memory_space=pl.ANY), vmem),
            scratch_shapes=[
                pltpu.VMEM((SLOTS, FACE, 128), f32), pltpu.VMEM((SLOTS, INNER, 128), f32),
                pltpu.VMEM((HOPS, FACE, 128), f32), pltpu.VMEM((HOPS, FACE, 128), f32),
                pltpu.VMEM((HOPS, INNER, 128), f32), pltpu.VMEM((HOPS, INNER, 128), f32),
                pltpu.VMEM((3 * PATCHES, FACE, 128), f32), pltpu.VMEM((160, 128), f32),
                pltpu.VMEM((160, 128), f32), pltpu.VMEM((160, 128), f32),
                pltpu.VMEM((480, 128), f32),
                pltpu.VMEM((nx * 16, 128), f32), pltpu.VMEM((nz * 16, 128), f32), pltpu.VMEM(((nz - 1) * 16, 128), f32),
                pltpu.VMEM((640, 128), f32),
                dma(HOPS), dma(HOPS), dma(HOPS), dma(HOPS), dma(2), dma(2),
                dma(nx - 1), dma(nx - 1), dma(nz - 1), dma(nz - 1), pltpu.SemaphoreType.DMA,
            ],
            compiler_params=pltpu.CompilerParams(collective_id=0, has_side_effects=True),
        )(blocks, dest_dev, dest_slot, neighbours, coarse_map)
        advanced = advanced.reshape(FIELDS, 32, PATCHES, 128).transpose(2, 0, 1, 3).reshape(PATCHES, FIELDS, 4096)
        return advanced, registers.reshape(1, FIELDS, 256)

    in_specs = (P(("grp", "dev"), None, None), P("grp"), P("grp"), P(None, "grp"), P("dev", None))
    out_specs = (P(("grp", "dev"), None, None), P(("grp", "dev"), None, None))
    return jax.shard_map(local, mesh=mesh, in_specs=in_specs, out_specs=out_specs, check_vma=False)
```

time: 75 us -> 41.7 us (0.56)
  the two profiles are of different devices: /device:TPU:25 before, /device:TPU:2 now
where the time goes in v1:
time: 41.7 us; the launch traced here: 41.4 us
  Pallas kernels  37.8 us (91%)
  local copies, waits for them, and re-layouts  3.02 us (7%)
  between operations  0.64 us (2%)
    pallas_call x1, Pallas kernels, local(): pl.pallas_call(functools.partial(kernel, nz, nx, n_dev), out_shape=(jax.S...  37.8 us
    unnamed x1, local copies, waits for them, and re-layouts  1.72 us
    reshape x1, local copies, waits for them, and re-layouts, local(): return (advanced, registers.reshape(1, FIELDS, 256))  1.3 us

profile of v1, /device:TPU:2, one launch (start us, length us, event | category | flops | bytes accessed | tf_op | source)
XLA Modules:
  0.0 41.4 jit_solution(11766908930377453283)
XLA Ops:
  0.6 37.8 %shard_map.68 = (f32[640,128]{1,0:T(8,128)}, f32[10,128]{1,0:T(8,128)}) custom-call(f32[1280,128]{1,0:T(8,128)} %bitcast.10, s32[128]{0:T(128)} %ddev.1, s32[128]{0:T(128)} %dslot.1, s32[2,64]{1,0:T(2,128)} %nbr.1, s32[1,192]{1,0:T(1,128)} %cmap.1), custom_call_target="tpu_custom_call" | custom-call | tf_op jit(solution)/shard_map/pallas_call | solution.py:313
  38.4 1.3 %reshape.24 = f32[1,5,256]{2,0,1:T(1,128)} reshape(f32[10,128]{1,0:T(8,128)} %get-tuple-element.5) | data formatting | bytes 10240 | tf_op jit(solution)/shard_map/reshape | solution.py:333
  39.7 1.7 %copy.12 = f32[4,5,4096]{2,0,1:T(4,128)} copy(f32[4,5,4096]{2,0,1:T(4,128)} %bitcast.11) | data formatting | bytes 655360

commit v2 on v1

--- a/solution.py
+++ b/solution.py
@@ -61,12 +61,19 @@
 
 def kernel(
     nz, nx, n_dev,
+    blk_hbm, ddev_hbm, dslot_hbm, nbr_hbm, cmap_hbm,
+    adv, reg,
     blk, ddev, dslot, nbr, cmap,
-    adv, reg,
     slot_face, slot_inner, face_send, face_recv, inner_send, inner_recv, near, outer, lower, upper, inner,
-    xpool, zbuf, zrecv, adv_buf,
-    face_ss, face_rs, inner_ss, inner_rs, ghost_ss, ghost_rs, x_ss, x_rs, z_ss, z_rs, out_sem,
+    xpool, zbuf, zrecv,
+    face_ss, face_rs, inner_ss, inner_rs, ghost_ss, ghost_rs, x_ss, x_rs, z_ss, z_rs, in_sem,
 ):
+    loads = []
+    for n, (source, held) in enumerate(
+        ((ddev_hbm, ddev), (blk_hbm, blk), (dslot_hbm, dslot), (nbr_hbm, nbr), (cmap_hbm, cmap))):
+        copy = pltpu.make_async_copy(source, held, in_sem.at[n])
+        copy.start()
+        loads.append(copy)
     me = lax.axis_index("dev")
     grp = lax.axis_index("grp")
     mz, mx = grp // nx, grp % nx
@@ -82,6 +89,8 @@
     for by in range(1, nz):
         pl.semaphore_signal(barrier, inc=1, device_id=z_at(by), device_id_type=MESH)
 
+    for copy in loads:
+        copy.wait()
     for j in range(SLOTS):
         for f in range(FIELDS):
             for part, first in ((0, 0), (4, 28)):
@@ -131,21 +140,27 @@
     for k in range(HOPS):
         inner_send[k] = slot_inner[going[k]]
 
-    lane32 = iota((8, 8 * nx), 1)
-    row8 = iota((8, 8 * nx), 0)
-    target = jnp.zeros((8, 8 * nx), jnp.int32)
+    width = 8 * nx
+    column = iota((8, 4 * width), 1)
+    target = jnp.zeros((8, 4 * width), jnp.int32)
     for i in range(nx):
         source = mz * nx + lax.rem(mx - i + nx, nx)
         for q in range(PATCHES):
-            at = (lane32 >> 3 == i) & ((lane32 & 3) == q)
+            at = (((column & (width - 1)) >> 3) == i) & ((column & 3) == q)
             target = jnp.where(at, cmap[0, source * PATCHES + q], target)
-    same_half = (row8 >> 2) == ((lane32 >> 2) & 1)
+    row8 = iota((8, width), 0)
+    same_half = (row8 >> 2) == ((iota((8, width), 1) >> 2) & 1)
     route = []
     for i in range(nz):
         code = (lax.rem(mz + i, nz) * nx + mx) * PATCHES
-        hit = (target == code + (row8 & 3)) & same_half
-        route.append(jnp.where(hit, 1.0, 0.0))
+        route.append(jnp.where((target[:, :width] == code + (row8 & 3)) & same_half, 1.0, 0.0))
     route = jnp.concatenate(route, axis=0)
+    wide_row, wide_column = iota((2 * nz, 4 * width), 0), iota((2 * nz, 4 * width), 1)
+    place_z = mz + (wide_row >> 1)
+    place_z = jnp.where(place_z >= nz, place_z - nz, place_z)
+    code = (place_z * nx + mx) * PATCHES + sum((wide_column >= t * width).astype(jnp.int32) for t in range(1, 4))
+    wide_target = jnp.broadcast_to(target[0:1], (2 * nz, 4 * width))
+    wide_route = jnp.where((wide_target == code) & ((wide_row & 1) == ((wide_column >> 2) & 1)), 1.0, 0.0)
 
     for copy in face_copies:
         copy.wait_recv()
@@ -224,15 +239,19 @@
 
     for copy in x_copies:
         copy.wait_recv()
-    for v in range(2):
-        pool = jnp.concatenate([xpool[i * 16 + v * 8:i * 16 + v * 8 + 8, :] for i in range(nx)], axis=0)
-        routed = jnp.dot(route, pool, precision=HIGHEST, preferred_element_type=jnp.float32)
-        for i in range(nz):
-            zbuf[i * 16 + v * 8:i * 16 + v * 8 + 8, :] = routed[i * 8:i * 8 + 8]
+    pool = jnp.concatenate([xpool[i * 16:i * 16 + 8, :] for i in range(nx)], axis=0)
+    routed = jnp.dot(route, pool, precision=HIGHEST, preferred_element_type=jnp.float32)
+    pool = jnp.concatenate([xpool[i * 16 + 8:i * 16 + 16, :] for i in range(nx)], axis=0)
+    group = iota((width, 128), 1) >> 5
+    pool = jnp.concatenate([jnp.where(group == t, pool, 0.0) for t in range(4)], axis=0)
+    routed_fifth = jnp.dot(wide_route, pool, precision=HIGHEST, preferred_element_type=jnp.float32)
+    for i in range(nz):
+        zbuf[i, 0:8, :] = routed[i * 8:i * 8 + 8]
+        zbuf[i, 8:10, :] = routed_fifth[i * 2:i * 2 + 2]
     z_copies = []
-    for i in range(1, nz):
-        copy = pltpu.make_async_remote_copy(
-            src_ref=zbuf.at[pl.ds(i * 16, 16)], dst_ref=zrecv.at[pl.ds((i - 1) * 16, 16)],
+    for i in sorted(range(1, nz), key=lambda i: -min(i, nz - i)):
+        copy = pltpu.make_async_remote_copy(
+            src_ref=zbuf.at[i, pl.ds(0, 10)], dst_ref=zrecv.at[i - 1, pl.ds(0, 10)],
             send_sem=z_ss.at[i - 1], recv_sem=z_rs.at[i - 1], device_id=z_at(i), device_id_type=MESH)
         copy.start()
         z_copies.append(copy)
@@ -268,35 +287,31 @@
         if x > 0:
             u = layer(x - 1)
             for f in range(FIELDS):
-                adv_buf[pl.ds(f * 128 + (x - 1) * 8, 8), :] = u[f] - COURANT * (flux[f] - below_flux[f])
+                adv[pl.ds(f * 128 + (x - 1) * 8, 8), :] = u[f] - COURANT * (flux[f] - below_flux[f])
         here, above, slope, below_flux = above, beyond, slope_above, flux
-    out = pltpu.make_async_copy(adv_buf, adv, out_sem)
-    out.start()
 
     for copy in z_copies:
         copy.wait_recv()
-    totals = []
-    for v in range(2):
-        total = zbuf[v * 8:v * 8 + 8, :]
-        for i in range(nz - 1):
-            total = total + zrecv[i * 16 + v * 8:i * 16 + v * 8 + 8, :]
-        totals.append(total)
-    parts = [jnp.where(lane8 >> 5 == f, totals[0], 0.0) for f in range(4)]
-    parts.append(jnp.where(lane8 >> 5 == 0, totals[1], 0.0))
+    total, fifth = zbuf[0, 0:8, :], zbuf[0, 8:10, :]
+    for i in range(nz - 1):
+        total = total + zrecv[i, 0:8, :]
+        fifth = fifth + zrecv[i, 8:10, :]
+    row = iota((8, 128), 0)
+    fifth = jnp.where(row < 4, fifth[0:1], fifth[1:2])
+    parts = [jnp.where(lane8 >> 5 == f, total, 0.0) for f in range(4)]
+    parts.append(jnp.where(lane8 >> 5 == row & 3, fifth, 0.0))
     place = jnp.where(
         (lane_in & 31) == ((lane_out >> 4) & 3) * 8 + (lane_out & 7), 1.0, 0.0)
     wide = jnp.dot(jnp.concatenate(parts, axis=0), place, precision=HIGHEST, preferred_element_type=jnp.float32)
-    row = iota((8, 128), 0)
     inside = (row >> 2 == lane8 >> 6) & ((row & 1) == ((lane8 >> 3) & 1))
     for f in range(FIELDS):
         block = wide[f * 8:f * 8 + 8]
         for half in range(2):
             chosen = jnp.where(inside & ((row & 3) >> 1 == half), block, 0.0)
-            reg[pl.ds(f * 2 + half, 1), :] = jnp.sum(chosen, axis=0, keepdims=True)
+            reg[f, :, pl.ds(half * 128, 128)] = jnp.sum(chosen, axis=0, keepdims=True)
 
     for copy in face_copies + ghost_copies + inner_copies + x_copies + z_copies:
         copy.wait_send()
-    out.wait()
 
 
 def solution(mesh):
@@ -307,30 +322,31 @@
     def local(block_states, dest_dev, dest_slot, neighbours, coarse_map):
         blocks = block_states.reshape(SLOTS, FIELDS, 32, 128).transpose(1, 2, 0, 3).reshape(FIELDS * 32 * SLOTS, 128)
         vmem = pl.BlockSpec(memory_space=pltpu.VMEM)
-        smem = pl.BlockSpec(memory_space=pltpu.SMEM)
+        hbm = pl.BlockSpec(memory_space=pltpu.HBM)
         f32 = jnp.float32
         dma = lambda n: pltpu.SemaphoreType.DMA((n,))
         advanced, registers = pl.pallas_call(
             functools.partial(kernel, nz, nx, n_dev),
-            out_shape=(jax.ShapeDtypeStruct((640, 128), f32), jax.ShapeDtypeStruct((10, 128), f32)),
-            in_specs=[vmem, smem, smem, smem, smem],
-            out_specs=(pl.BlockSpec(memory_space=pl.ANY), vmem),
+            out_shape=(pltpu.VMEM((640, 128), f32), pltpu.VMEM((FIELDS, 1, 256), f32)),
+            in_specs=[hbm] * 5,
+            out_specs=(vmem, vmem),
             scratch_shapes=[
+                pltpu.VMEM((1280, 128), f32), pltpu.SMEM(dest_dev.shape, jnp.int32), pltpu.SMEM(dest_slot.shape, jnp.int32),
+                pltpu.SMEM(neighbours.shape, jnp.int32), pltpu.SMEM(coarse_map.shape, jnp.int32),
                 pltpu.VMEM((SLOTS, FACE, 128), f32), pltpu.VMEM((SLOTS, INNER, 128), f32),
                 pltpu.VMEM((HOPS, FACE, 128), f32), pltpu.VMEM((HOPS, FACE, 128), f32),
                 pltpu.VMEM((HOPS, INNER, 128), f32), pltpu.VMEM((HOPS, INNER, 128), f32),
                 pltpu.VMEM((3 * PATCHES, FACE, 128), f32), pltpu.VMEM((160, 128), f32),
                 pltpu.VMEM((160, 128), f32), pltpu.VMEM((160, 128), f32),
                 pltpu.VMEM((480, 128), f32),
-                pltpu.VMEM((nx * 16, 128), f32), pltpu.VMEM((nz * 16, 128), f32), pltpu.VMEM(((nz - 1) * 16, 128), f32),
-                pltpu.VMEM((640, 128), f32),
+                pltpu.VMEM((nx * 16, 128), f32), pltpu.VMEM((nz, 16, 128), f32), pltpu.VMEM((nz - 1, 16, 128), f32),
                 dma(HOPS), dma(HOPS), dma(HOPS), dma(HOPS), dma(2), dma(2),
-                dma(nx - 1), dma(nx - 1), dma(nz - 1), dma(nz - 1), pltpu.SemaphoreType.DMA,
+                dma(nx - 1), dma(nx - 1), dma(nz - 1), dma(nz - 1), dma(5),
             ],
-            compiler_params=pltpu.CompilerParams(collective_id=0, has_side_effects=True),
-        )(blocks, dest_dev, dest_slot, neighbours, coarse_map)
+            compiler_params=pltpu.CompilerParams(collective_id=0, has_side_effects=True, vmem_limit_bytes=24 * 1024 * 1024),
+        )(*[pltpu.with_memory_space_constraint(a, pltpu.HBM) for a in (blocks, dest_dev, dest_slot, neighbours, coarse_map)])
         advanced = advanced.reshape(FIELDS, 32, PATCHES, 128).transpose(2, 0, 1, 3).reshape(PATCHES, FIELDS, 4096)
-        return advanced, registers.reshape(1, FIELDS, 256)
+        return advanced, registers.transpose(1, 0, 2)
 
     in_specs = (P(("grp", "dev"), None, None), P("grp"), P("grp"), P(None, "grp"), P("dev", None))
     out_specs = (P(("grp", "dev"), None, None), P(("grp", "dev"), None, None))

time: 41.7 us -> 37.5 us (0.90)
  the two profiles are of different devices: /device:TPU:2 before, /device:TPU:1 now
where the time goes in v2:
time: 37.5 us; the launch traced here: 37.3 us
  Pallas kernels  35.4 us (94%)
  local copies, waits for them, and re-layouts  1.32 us (4%)
  between operations  0.64 us (2%)
    pallas_call x1, Pallas kernels, local(): pl.pallas_call(functools.partial(kernel, nz, nx, n_dev), out_shape=(pltpu...  35.4 us
    unnamed x2, local copies, waits for them, and re-layouts  1.32 us

profile of v2, /device:TPU:1, one launch (start us, length us, event | category | flops | bytes accessed | tf_op | source)
XLA Modules:
  0.0 37.3 jit_solution(11302250572348044544)
XLA Ops:
  0.6 35.4 %shard_map.68 = (f32[640,128]{1,0:T(8,128)S(1)}, f32[5,1,256]{2,1,0:T(1,128)S(1)}) custom-call(f32[1280,128]{1,0:T(8,128)} %bitcast.13, s32[128]{0:T(128)} %ddev_hbm.1, s32[128]{0:T(128)} %dslot_hbm.1, s32[2,64]{1,0:T(2,128)} %nbr_hbm.1, s32[1,192]{1,0:T(1,128)} %cmap_hbm.1), custom_call_target="tpu_custom_call" | custom-call | tf_op jit(solution)/shard_map/pallas_call | solution.py:328
  36.0 0.7 %copy.10 = f32[4,5,4096]{2,0,1:T(4,128)} copy(f32[4,5,4096]{2,0,1:T(4,128)S(1)} %bitcast.11) | data formatting | bytes 655360
  36.7 0.6 %copy.11 = f32[1,5,256]{2,0,1:T(1,128)} copy(f32[1,5,256]{2,0,1:T(1,128)S(1)} %bitcast.12) | data formatting | bytes 10240

commit v3 on v2

--- a/solution.py
+++ b/solution.py
@@ -17,8 +17,22 @@
 HIGHEST = lax.Precision.HIGHEST
 HOPS = 3
 
-FACE = 40
+EDGE = 20
 INNER = 120
+
+AHEAD = (
+    (4, 13, (("low", 3),)),
+    (3, 10, (("low", 2), ("low", 3), ("high", 3))),
+    (2, 6, (("low", 1), ("low", 2), ("low", 3), ("high", 2))),
+    (1, 0, (("kept", 1), ("kept", 2), ("kept", 3), ("low", 1), ("low", 2), ("high", 1))),
+    (-1, 14, (("kept", 0), ("kept", 1), ("kept", 2))),
+)
+SENT = 17
+OWN = SENT
+ENTRIES = SENT + PATCHES + 1
+LOW_AT = ((None, 6, 10, 13), (None, 3, 7, 11), (None, OWN + PATCHES, 4, 8))
+LOW_KEPT = (-1, OWN, 14)
+HIGH_AT = (None, 5, 9, 12)
 
 
 def primitives(u):
@@ -63,14 +77,17 @@
     nz, nx, n_dev,
     blk_hbm, ddev_hbm, dslot_hbm, nbr_hbm, cmap_hbm,
     adv, reg,
-    blk, ddev, dslot, nbr, cmap,
-    slot_face, slot_inner, face_send, face_recv, inner_send, inner_recv, near, outer, lower, upper, inner,
+    blk, ddev, dslot, nbr, cmap, table,
+    slot_low, slot_high, slot_inner, edge_send, edges, inner_send, inner_recv, near, low, high, lower, upper, inner,
     xpool, zbuf, zrecv,
-    face_ss, face_rs, inner_ss, inner_rs, ghost_ss, ghost_rs, x_ss, x_rs, z_ss, z_rs, in_sem,
+    edge_ss, edge_rs, inner_ss, inner_rs, ghost_ss, ghost_rs, x_ss, x_rs, z_ss, z_rs, in_sem,
 ):
     loads = []
-    for n, (source, held) in enumerate(
-        ((ddev_hbm, ddev), (blk_hbm, blk), (dslot_hbm, dslot), (nbr_hbm, nbr), (cmap_hbm, cmap))):
+    top, bottom, middle = pl.ds(28 * SLOTS, 4 * SLOTS), pl.ds(0, 4 * SLOTS), pl.ds(4 * SLOTS, 24 * SLOTS)
+    for n, (source, held) in enumerate((
+        (ddev_hbm, ddev), (dslot_hbm, dslot),
+        (blk_hbm.at[:, bottom], blk.at[:, bottom]), (blk_hbm.at[:, top], blk.at[:, top]),
+        (nbr_hbm, nbr), (cmap_hbm, cmap), (blk_hbm.at[:, middle], blk.at[:, middle]))):
         copy = pltpu.make_async_copy(source, held, in_sem.at[n])
         copy.start()
         loads.append(copy)
@@ -82,41 +99,22 @@
     z_at = lambda by: {"grp": lax.rem(mz + by, nz) * nx + mx}
 
     barrier = pltpu.get_barrier_semaphore()
-    for by in (-1, -2, -3, 1):
+    for by in (-1, 1, -2, -3, -4):
         pl.semaphore_signal(barrier, inc=1, device_id=dev_at(by), device_id_type=MESH)
     for by in range(1, nx):
         pl.semaphore_signal(barrier, inc=1, device_id=x_at(by), device_id_type=MESH)
     for by in range(1, nz):
         pl.semaphore_signal(barrier, inc=1, device_id=z_at(by), device_id_type=MESH)
 
-    for copy in loads:
-        copy.wait()
-    for j in range(SLOTS):
-        for f in range(FIELDS):
-            for part, first in ((0, 0), (4, 28)):
-                slot_face[j, pl.ds(f * 8 + part, 4), :] = blk[
-                    pl.ds((f * 32 + first) * SLOTS + j, 4, stride=SLOTS), :]
-
-    going = []
+    loads[0].wait()
+    loads[1].wait()
+    going = [None]
     for k in range(1, HOPS + 1):
         target = lax.rem(me + k, n_dev)
         slot = jnp.int32(0)
         for j in range(SLOTS):
             slot = jnp.where(ddev[me * SLOTS + j] == target, j, slot)
         going.append(slot)
-    for k in range(HOPS):
-        face_send[k] = slot_face[going[k]]
-
-    pl.semaphore_wait(barrier, 4 + (nx - 1) + (nz - 1))
-
-    face_copies = []
-    for k in range(HOPS):
-        copy = pltpu.make_async_remote_copy(
-            src_ref=face_send.at[k], dst_ref=face_recv.at[k],
-            send_sem=face_ss.at[k], recv_sem=face_rs.at[k], device_id=dev_at(k + 1), device_id_type=MESH)
-        copy.start()
-        face_copies.append(copy)
-
     own_slot = []
     for q in range(PATCHES):
         slot = jnp.int32(0)
@@ -124,21 +122,70 @@
             i = me * SLOTS + j
             slot = jnp.where((ddev[i] == me) & (dslot[i] == q), j, slot)
         own_slot.append(slot)
-    origin = [jnp.int32(0)] * PATCHES
-    for k in range(1, HOPS + 1):
-        source = lax.rem(me - k + n_dev, n_dev)
-        landing = jnp.int32(-1)
-        for j in range(SLOTS):
-            i = source * SLOTS + j
-            landing = jnp.where(ddev[i] == me, dslot[i], landing)
-        for q in range(PATCHES):
-            origin[q] = jnp.where(landing == q, k, origin[q])
-
+
+    loads[2].wait()
+    loads[3].wait()
     for j in range(SLOTS):
         for f in range(FIELDS):
-            slot_inner[j, pl.ds(f * 24, 24), :] = blk[pl.ds((f * 32 + 4) * SLOTS + j, 24, stride=SLOTS), :]
-    for k in range(HOPS):
-        inner_send[k] = slot_inner[going[k]]
+            slot_low[j, pl.ds(f * 4, 4), :] = blk[f, pl.ds(j, 4, stride=SLOTS), :]
+            slot_high[j, pl.ds(f * 4, 4), :] = blk[f, pl.ds(28 * SLOTS + j, 4, stride=SLOTS), :]
+    for _, first, entries in AHEAD:
+        for n, (what, j) in enumerate(entries):
+            if what == "high":
+                edge_send[first + n] = slot_high[going[j]]
+            else:
+                edge_send[first + n] = slot_low[own_slot[j] if what == "kept" else going[j]]
+
+    pl.semaphore_wait(barrier, 5 + (nx - 1) + (nz - 1))
+
+    edge_copies = []
+    for n, (by, first, entries) in enumerate(AHEAD):
+        part = pl.ds(first, len(entries))
+        copy = pltpu.make_async_remote_copy(
+            src_ref=edge_send.at[part], dst_ref=edges.at[part],
+            send_sem=edge_ss.at[n], recv_sem=edge_rs.at[n], device_id=dev_at(by), device_id_type=MESH)
+        copy.start()
+        edge_copies.append(copy)
+
+    for q in range(PATCHES):
+        edges[OWN + q] = slot_low[own_slot[q]]
+    edges[OWN + PATCHES] = slot_low[going[1]]
+    origin = [jnp.int32(0)] * PATCHES
+    high_at = [jnp.int32(0)] * PATCHES
+    low_at = []
+    for beside in range(3):
+        place = lax.rem(me + beside - 1 + n_dev, n_dev)
+        at = [jnp.int32(min(max(LOW_KEPT[beside] + q, 0), ENTRIES - 1)) for q in range(PATCHES)]
+        for k in range(1, HOPS + 1):
+            source = lax.rem(place - k + n_dev, n_dev)
+            landing = jnp.int32(-1)
+            for j in range(SLOTS):
+                i = source * SLOTS + j
+                landing = jnp.where(ddev[i] == place, dslot[i], landing)
+            for q in range(PATCHES):
+                at[q] = jnp.where(landing == q, LOW_AT[beside][k], at[q])
+                if beside == 1:
+                    origin[q] = jnp.where(landing == q, k, origin[q])
+                    high_at[q] = jnp.where(landing == q, HIGH_AT[k], high_at[q])
+        for q in range(PATCHES):
+            table[beside * PATCHES + q] = at[q]
+        low_at.append(at)
+    loads[4].wait()
+    lower_nbr = [nbr[0, me * PATCHES + q] for q in range(PATCHES)]
+    upper_nbr = [nbr[1, me * PATCHES + q] for q in range(PATCHES)]
+
+    def place_of(nb, q):
+        place = jnp.where(nb < 0, PATCHES + q, nb - (me - 1) * PATCHES)
+        return jnp.minimum(jnp.maximum(place, 0), 3 * PATCHES - 1)
+
+    above_at = [table[place_of(upper_nbr[q], q)] for q in range(PATCHES)]
+    patch = iota((8, 128), 0) & 3
+    lower_ids = jnp.zeros((8, 128), jnp.int32)
+    upper_ids = jnp.zeros((8, 128), jnp.int32)
+    for q in range(PATCHES):
+        lower_ids = jnp.where(patch == q, lower_nbr[q], lower_ids)
+        upper_ids = jnp.where(patch == q, upper_nbr[q], upper_ids)
+    loads[5].wait()
 
     width = 8 * nx
     column = iota((8, 4 * width), 1)
@@ -162,53 +209,21 @@
     wide_target = jnp.broadcast_to(target[0:1], (2 * nz, 4 * width))
     wide_route = jnp.where((wide_target == code) & ((wide_row & 1) == ((wide_column >> 2) & 1)), 1.0, 0.0)
 
-    for copy in face_copies:
-        copy.wait_recv()
-    for q in range(PATCHES):
-        arrived = jnp.maximum(origin[q] - 1, 0)
-        face = jnp.where(origin[q] > 0, face_recv[arrived], slot_face[own_slot[q]])
-        near[PATCHES + q] = face
-        outer[pl.ds(q, FACE, stride=PATCHES), :] = face
-
-    ghost_copies = []
-    for n, (by, first, to) in enumerate(((1, 1, 1), (-1, 0, 2 * PATCHES))):
-        copy = pltpu.make_async_remote_copy(
-            src_ref=near.at[pl.ds(PATCHES + first, 3)], dst_ref=near.at[pl.ds(to, 3)],
-            send_sem=ghost_ss.at[n], recv_sem=ghost_rs.at[n], device_id=dev_at(by), device_id_type=MESH)
-        copy.start()
-        ghost_copies.append(copy)
-    inner_copies = []
-    for k in range(HOPS):
-        copy = pltpu.make_async_remote_copy(
-            src_ref=inner_send.at[k], dst_ref=inner_recv.at[k],
-            send_sem=inner_ss.at[k], recv_sem=inner_rs.at[k], device_id=dev_at(k + 1), device_id_type=MESH)
-        copy.start()
-        inner_copies.append(copy)
-
-    patch = iota((8, 128), 0) & 3
-    lower_nbr = [nbr[0, me * PATCHES + q] for q in range(PATCHES)]
-    upper_nbr = [nbr[1, me * PATCHES + q] for q in range(PATCHES)]
-    lower_ids = jnp.zeros((8, 128), jnp.int32)
-    upper_ids = jnp.zeros((8, 128), jnp.int32)
-    for q in range(PATCHES):
-        lower_ids = jnp.where(patch == q, lower_nbr[q], lower_ids)
-        upper_ids = jnp.where(patch == q, upper_nbr[q], upper_ids)
-
-    def neighbour(nb, q):
-        place = jnp.where(nb < 0, PATCHES + q, nb - (me - 1) * PATCHES)
-        return near[jnp.minimum(jnp.maximum(place, 0), 3 * PATCHES - 1)]
-
-    for copy in ghost_copies:
-        copy.wait_recv()
-    for q in range(PATCHES):
-        upper[pl.ds(q, FACE, stride=PATCHES), :] = neighbour(upper_nbr[q], q)
-
-    own = lambda side, layer, f: outer[pl.ds(f * 32 + side * 16 + layer * 8, 8), :]
-    last = [own(1, 1, f) for f in range(FIELDS)]
+    for copy in edge_copies:
+        copy.wait_recv()
+    for q in range(PATCHES):
+        edge = jnp.where(origin[q] > 0, edges[high_at[q]], slot_high[own_slot[q]])
+        near[PATCHES + q] = edge
+        high[pl.ds(q, EDGE, stride=PATCHES), :] = edge
+        upper[pl.ds(q, EDGE, stride=PATCHES), :] = edges[above_at[q]]
+
+    def outer(side, layer):
+        return [side[pl.ds(f * 16 + layer * 8, 8), :] for f in range(FIELDS)]
+
+    last = outer(high, 1)
     ghosts_above = [
-        [jnp.where(upper_ids < 0, last[f], upper[pl.ds(f * 32 + layer * 8, 8), :]) for f in range(FIELDS)]
-        for layer in range(2)]
-    p14 = primitives([own(1, 0, f) for f in range(FIELDS)])
+        [jnp.where(upper_ids < 0, a, b) for a, b in zip(last, outer(upper, layer))] for layer in range(2)]
+    p14 = primitives(outer(high, 0))
     p15 = primitives(last)
     p16 = primitives(ghosts_above[0])
     p17 = primitives(ghosts_above[1])
@@ -234,8 +249,25 @@
         copy.start()
         x_copies.append(copy)
 
-    for q in range(PATCHES):
-        lower[pl.ds(q, FACE, stride=PATCHES), :] = neighbour(lower_nbr[q], q)
+    ghost_copies = []
+    for n, (by, first, to) in enumerate(((1, 1, 1), (-1, 0, 2 * PATCHES))):
+        copy = pltpu.make_async_remote_copy(
+            src_ref=near.at[pl.ds(PATCHES + first, 3)], dst_ref=near.at[pl.ds(to, 3)],
+            send_sem=ghost_ss.at[n], recv_sem=ghost_rs.at[n], device_id=dev_at(by), device_id_type=MESH)
+        copy.start()
+        ghost_copies.append(copy)
+    loads[6].wait()
+    for j in range(SLOTS):
+        for f in range(FIELDS):
+            slot_inner[j, pl.ds(f * 24, 24), :] = blk[f, pl.ds(4 * SLOTS + j, 24, stride=SLOTS), :]
+    inner_copies = []
+    for k in range(HOPS):
+        inner_send[k] = slot_inner[going[k + 1]]
+        copy = pltpu.make_async_remote_copy(
+            src_ref=inner_send.at[k], dst_ref=inner_recv.at[k],
+            send_sem=inner_ss.at[k], recv_sem=inner_rs.at[k], device_id=dev_at(k + 1), device_id_type=MESH)
+        copy.start()
+        inner_copies.append(copy)
 
     for copy in x_copies:
         copy.wait_recv()
@@ -256,6 +288,11 @@
         copy.start()
         z_copies.append(copy)
 
+    for copy in ghost_copies:
+        copy.wait_recv()
+    for q in range(PATCHES):
+        low[pl.ds(q, EDGE, stride=PATCHES), :] = edges[low_at[1][q]]
+        lower[pl.ds(q, EDGE, stride=PATCHES), :] = near[place_of(lower_nbr[q], q)]
     for copy in inner_copies:
         copy.wait_recv()
     for q in range(PATCHES):
@@ -265,16 +302,15 @@
             theirs = inner_recv[arrived, pl.ds(f * 24, 24), :]
             inner[pl.ds(f * 96 + q, 24, stride=PATCHES), :] = jnp.where(origin[q] > 0, theirs, mine)
 
-    first = [own(0, 0, f) for f in range(FIELDS)]
+    first = outer(low, 0)
     ghosts_below = [
-        [jnp.where(lower_ids < 0, first[f], lower[pl.ds(f * 32 + 16 + layer * 8, 8), :]) for f in range(FIELDS)]
-        for layer in range(2)]
+        [jnp.where(lower_ids < 0, a, b) for a, b in zip(first, outer(lower, layer))] for layer in range(2)]
 
     def layer(x):
         if x < 2:
-            return [own(0, x, f) for f in range(FIELDS)]
+            return outer(low, x)
         if x >= 14:
-            return [own(1, x - 14, f) for f in range(FIELDS)]
+            return outer(high, x - 14)
         return [inner[pl.ds(f * 96 + (x - 2) * 8, 8), :] for f in range(FIELDS)]
 
     here, above = primitives(ghosts_below[1]), primitives(first)
@@ -310,7 +346,7 @@
             chosen = jnp.where(inside & ((row & 3) >> 1 == half), block, 0.0)
             reg[f, :, pl.ds(half * 128, 128)] = jnp.sum(chosen, axis=0, keepdims=True)
 
-    for copy in face_copies + ghost_copies + inner_copies + x_copies + z_copies:
+    for copy in edge_copies + ghost_copies + inner_copies + x_copies + z_copies:
         copy.wait_send()
 
 
@@ -320,7 +356,7 @@
     nz = n_grp // nx
 
     def local(block_states, dest_dev, dest_slot, neighbours, coarse_map):
-        blocks = block_states.reshape(SLOTS, FIELDS, 32, 128).transpose(1, 2, 0, 3).reshape(FIELDS * 32 * SLOTS, 128)
+        blocks = block_states.reshape(SLOTS, FIELDS, 32, 128).transpose(1, 2, 0, 3).reshape(FIELDS, 32 * SLOTS, 128)
         vmem = pl.BlockSpec(memory_space=pltpu.VMEM)
         hbm = pl.BlockSpec(memory_space=pltpu.HBM)
         f32 = jnp.float32
@@ -331,17 +367,19 @@
             in_specs=[hbm] * 5,
             out_specs=(vmem, vmem),
             scratch_shapes=[
-                pltpu.VMEM((1280, 128), f32), pltpu.SMEM(dest_dev.shape, jnp.int32), pltpu.SMEM(dest_slot.shape, jnp.int32),
+                pltpu.VMEM((FIELDS, 32 * SLOTS, 128), f32), pltpu.SMEM(dest_dev.shape, jnp.int32), pltpu.SMEM(dest_slot.shape, jnp.int32),
                 pltpu.SMEM(neighbours.shape, jnp.int32), pltpu.SMEM(coarse_map.shape, jnp.int32),
-                pltpu.VMEM((SLOTS, FACE, 128), f32), pltpu.VMEM((SLOTS, INNER, 128), f32),
-                pltpu.VMEM((HOPS, FACE, 128), f32), pltpu.VMEM((HOPS, FACE, 128), f32),
+                pltpu.SMEM((3 * PATCHES,), jnp.int32),
+                pltpu.VMEM((SLOTS, EDGE, 128), f32), pltpu.VMEM((SLOTS, EDGE, 128), f32),
+                pltpu.VMEM((SLOTS, INNER, 128), f32),
+                pltpu.VMEM((SENT, EDGE, 128), f32), pltpu.VMEM((ENTRIES, EDGE, 128), f32),
                 pltpu.VMEM((HOPS, INNER, 128), f32), pltpu.VMEM((HOPS, INNER, 128), f32),
-                pltpu.VMEM((3 * PATCHES, FACE, 128), f32), pltpu.VMEM((160, 128), f32),
-                pltpu.VMEM((160, 128), f32), pltpu.VMEM((160, 128), f32),
+                pltpu.VMEM((3 * PATCHES, EDGE, 128), f32), pltpu.VMEM((80, 128), f32), pltpu.VMEM((80, 128), f32),
+                pltpu.VMEM((80, 128), f32), pltpu.VMEM((80, 128), f32),
                 pltpu.VMEM((480, 128), f32),
-                pltpu.VMEM((nx * 16, 128), f32), pltpu.VMEM((nz, 16, 128), f32), pltpu.VMEM((nz - 1, 16, 128), f32),
-                dma(HOPS), dma(HOPS), dma(HOPS), dma(HOPS), dma(2), dma(2),
-                dma(nx - 1), dma(nx - 1), dma(nz - 1), dma(nz - 1), dma(5),
+                pltpu.VMEM((nx * 16, 128), f32), pltpu.VMEM((nz, 16, 128), f32), pltpu.VMEM((max(nz - 1, 1), 16, 128), f32),
+                dma(len(AHEAD)), dma(len(AHEAD)), dma(HOPS), dma(HOPS), dma(2), dma(2),
+                dma(max(nx - 1, 1)), dma(max(nx - 1, 1)), dma(max(nz - 1, 1)), dma(max(nz - 1, 1)), dma(7),
             ],
             compiler_params=pltpu.CompilerParams(collective_id=0, has_side_effects=True, vmem_limit_bytes=24 * 1024 * 1024),
         )(*[pltpu.with_memory_space_constraint(a, pltpu.HBM) for a in (blocks, dest_dev, dest_slot, neighbours, coarse_map)])

time: 37.5 us -> 35.6 us (0.949)
  the two profiles are of different devices: /device:TPU:1 before, /device:TPU:2 now
where the time goes in v3:
time: 35.6 us; the launch traced here: 35.5 us
  Pallas kernels  33.5 us (94%)
  local copies, waits for them, and re-layouts  1.32 us (4%)
  between operations  0.64 us (2%)
    pallas_call x1, Pallas kernels, local(): pl.pallas_call(functools.partial(kernel, nz, nx, n_dev), out_shape=(pltpu...  33.5 us
    unnamed x2, local copies, waits for them, and re-layouts  1.32 us

profile of v3, /device:TPU:2, one launch (start us, length us, event | category | flops | bytes accessed | tf_op | source)
XLA Modules:
  0.0 35.5 jit_solution(16368442415140737431)
XLA Ops:
  0.6 33.5 %shard_map.68 = (f32[640,128]{1,0:T(8,128)S(1)}, f32[5,1,256]{2,1,0:T(1,128)S(1)}) custom-call(f32[5,256,128]{2,1,0:T(8,128)} %bitcast.13, s32[128]{0:T(128)} %ddev_hbm.1, s32[128]{0:T(128)} %dslot_hbm.1, s32[2,64]{1,0:T(2,128)} %nbr_hbm.1, s32[1,192]{1,0:T(1,128)} %cmap_hbm.1), custom_call_target="tpu_custom_call" | custom-call | tf_op jit(solution)/shard_map/pallas_call | solution.py:364
  34.1 0.7 %copy.10 = f32[4,5,4096]{2,0,1:T(4,128)} copy(f32[4,5,4096]{2,0,1:T(4,128)S(1)} %bitcast.11) | data formatting | bytes 655360
  34.9 0.6 %copy.11 = f32[1,5,256]{2,0,1:T(1,128)} copy(f32[1,5,256]{2,0,1:T(1,128)S(1)} %bitcast.12) | data formatting | bytes 10240

commit v4 on v3

--- a/solution.py
+++ b/solution.py
@@ -80,7 +80,7 @@
     blk, ddev, dslot, nbr, cmap, table,
     slot_low, slot_high, slot_inner, edge_send, edges, inner_send, inner_recv, near, low, high, lower, upper, inner,
     xpool, zbuf, zrecv,
-    edge_ss, edge_rs, inner_ss, inner_rs, ghost_ss, ghost_rs, x_ss, x_rs, z_ss, z_rs, in_sem,
+    edge_ss, edge_rs, inner_ss, inner_rs, ghost_ss, ghost_rs, x_ss, x_rs, z_ss, z_rs, in_sem, ready,
 ):
     loads = []
     top, bottom, middle = pl.ds(28 * SLOTS, 4 * SLOTS), pl.ds(0, 4 * SLOTS), pl.ds(4 * SLOTS, 24 * SLOTS)
@@ -104,7 +104,9 @@
     for by in range(1, nx):
         pl.semaphore_signal(barrier, inc=1, device_id=x_at(by), device_id_type=MESH)
     for by in range(1, nz):
-        pl.semaphore_signal(barrier, inc=1, device_id=z_at(by), device_id_type=MESH)
+        @pl.when(mz + by < nz)
+        def _():
+            pl.semaphore_signal(barrier, inc=1, device_id=z_at(by), device_id_type=MESH)
 
     loads[0].wait()
     loads[1].wait()
@@ -136,7 +138,7 @@
             else:
                 edge_send[first + n] = slot_low[own_slot[j] if what == "kept" else going[j]]
 
-    pl.semaphore_wait(barrier, 5 + (nx - 1) + (nz - 1))
+    pl.semaphore_wait(barrier, 5 + (nx - 1) + mz)
 
     edge_copies = []
     for n, (by, first, entries) in enumerate(AHEAD):
@@ -146,6 +148,11 @@
             send_sem=edge_ss.at[n], recv_sem=edge_rs.at[n], device_id=dev_at(by), device_id_type=MESH)
         copy.start()
         edge_copies.append(copy)
+
+    for by in range(1, nz):
+        @pl.when(mz >= by)
+        def _():
+            pl.semaphore_signal(ready, inc=1, device_id=z_at(nz - by), device_id_type=MESH)
 
     for q in range(PATCHES):
         edges[OWN + q] = slot_low[own_slot[q]]
@@ -285,8 +292,8 @@
         copy = pltpu.make_async_remote_copy(
             src_ref=zbuf.at[i, pl.ds(0, 10)], dst_ref=zrecv.at[i - 1, pl.ds(0, 10)],
             send_sem=z_ss.at[i - 1], recv_sem=z_rs.at[i - 1], device_id=z_at(i), device_id_type=MESH)
-        copy.start()
-        z_copies.append(copy)
+        pl.when(mz + i >= nz)(copy.start)
+        z_copies.append((i, copy))
 
     for copy in ghost_copies:
         copy.wait_recv()
@@ -326,6 +333,12 @@
                 adv[pl.ds(f * 128 + (x - 1) * 8, 8), :] = u[f] - COURANT * (flux[f] - below_flux[f])
         here, above, slope, below_flux = above, beyond, slope_above, flux
 
+    @pl.when(mz < nz - 1)
+    def _():
+        pl.semaphore_wait(ready, nz - 1 - mz)
+        for i, copy in z_copies:
+            pl.when(mz + i < nz)(copy.start)
+    z_copies = [copy for _, copy in z_copies]
     for copy in z_copies:
         copy.wait_recv()
     total, fifth = zbuf[0, 0:8, :], zbuf[0, 8:10, :]
@@ -379,7 +392,7 @@
                 pltpu.VMEM((480, 128), f32),
                 pltpu.VMEM((nx * 16, 128), f32), pltpu.VMEM((nz, 16, 128), f32), pltpu.VMEM((max(nz - 1, 1), 16, 128), f32),
                 dma(len(AHEAD)), dma(len(AHEAD)), dma(HOPS), dma(HOPS), dma(2), dma(2),
-                dma(max(nx - 1, 1)), dma(max(nx - 1, 1)), dma(max(nz - 1, 1)), dma(max(nz - 1, 1)), dma(7),
+                dma(max(nx - 1, 1)), dma(max(nx - 1, 1)), dma(max(nz - 1, 1)), dma(max(nz - 1, 1)), dma(7), pltpu.SemaphoreType.REGULAR,
             ],
             compiler_params=pltpu.CompilerParams(collective_id=0, has_side_effects=True, vmem_limit_bytes=24 * 1024 * 1024),
         )(*[pltpu.with_memory_space_constraint(a, pltpu.HBM) for a in (blocks, dest_dev, dest_slot, neighbours, coarse_map)])

time: 35.6 us -> 32.1 us (0.902)
  the two profiles are of different devices: /device:TPU:2 before, /device:TPU:24 now
where the time goes in v4:
time: 32.1 us; the launch traced here: 31.9 us
  Pallas kernels  30 us (93%)
  local copies, waits for them, and re-layouts  1.32 us (4%)
  between operations  0.64 us (2%)
    pallas_call x1, Pallas kernels, local(): pl.pallas_call(functools.partial(kernel, nz, nx, n_dev), out_shape=(pltpu...  30 us
    unnamed x2, local copies, waits for them, and re-layouts  1.32 us

profile of v4, /device:TPU:24, one launch (start us, length us, event | category | flops | bytes accessed | tf_op | source)
XLA Modules:
  0.0 31.9 jit_solution(9231084728789464256)
XLA Ops:
  0.6 30.0 %shard_map.68 = (f32[640,128]{1,0:T(8,128)S(1)}, f32[5,1,256]{2,1,0:T(1,128)S(1)}) custom-call(f32[5,256,128]{2,1,0:T(8,128)} %bitcast.13, s32[128]{0:T(128)} %ddev_hbm.1, s32[128]{0:T(128)} %dslot_hbm.1, s32[2,64]{1,0:T(2,128)} %nbr_hbm.1, s32[1,192]{1,0:T(1,128)} %cmap_hbm.1), custom_call_target="tpu_custom_call" | custom-call | tf_op jit(solution)/shard_map/pallas_call | solution.py:377
  30.6 0.7 %copy.10 = f32[4,5,4096]{2,0,1:T(4,128)} copy(f32[4,5,4096]{2,0,1:T(4,128)S(1)} %bitcast.11) | data formatting | bytes 655360
  31.3 0.6 %copy.11 = f32[1,5,256]{2,0,1:T(1,128)} copy(f32[1,5,256]{2,0,1:T(1,128)S(1)} %bitcast.12) | data formatting | bytes 10240

commit v5 on v4

--- a/solution.py
+++ b/solution.py
@@ -76,12 +76,26 @@
 def kernel(
     nz, nx, n_dev,
     blk_hbm, ddev_hbm, dslot_hbm, nbr_hbm, cmap_hbm,
-    adv, reg,
+    adv, sums,
     blk, ddev, dslot, nbr, cmap, table,
     slot_low, slot_high, slot_inner, edge_send, edges, inner_send, inner_recv, near, low, high, lower, upper, inner,
     xpool, zbuf, zrecv,
     edge_ss, edge_rs, inner_ss, inner_rs, ghost_ss, ghost_rs, x_ss, x_rs, z_ss, z_rs, in_sem, ready,
 ):
+    me = lax.axis_index("dev")
+    grp = lax.axis_index("grp")
+    mz, mx = grp >> (nx.bit_length() - 1), grp & (nx - 1)
+    dev_of = lambda place: place & (n_dev - 1)
+    z_of = lambda by: jnp.where(mz + by >= nz, mz + (by - nz), mz + by)
+    dev_at = lambda by: (grp, dev_of(me + by))
+    x_at = lambda by: ((grp - mx) + ((mx + by) & (nx - 1)), me)
+    z_at = lambda by: (z_of(by) * nx + mx, me)
+
+    barrier = pltpu.get_barrier_semaphore()
+    for by in (-1, 1, -2, -3, -4):
+        pl.semaphore_signal(barrier, inc=1, device_id=dev_at(by), device_id_type=MESH)
+    for by in range(1, nx):
+        pl.semaphore_signal(barrier, inc=1, device_id=x_at(by), device_id_type=MESH)
     loads = []
     top, bottom, middle = pl.ds(28 * SLOTS, 4 * SLOTS), pl.ds(0, 4 * SLOTS), pl.ds(4 * SLOTS, 24 * SLOTS)
     for n, (source, held) in enumerate((
@@ -91,18 +105,6 @@
         copy = pltpu.make_async_copy(source, held, in_sem.at[n])
         copy.start()
         loads.append(copy)
-    me = lax.axis_index("dev")
-    grp = lax.axis_index("grp")
-    mz, mx = grp // nx, grp % nx
-    dev_at = lambda by: {"dev": lax.rem(me + by + n_dev, n_dev)}
-    x_at = lambda by: {"grp": mz * nx + lax.rem(mx + by, nx)}
-    z_at = lambda by: {"grp": lax.rem(mz + by, nz) * nx + mx}
-
-    barrier = pltpu.get_barrier_semaphore()
-    for by in (-1, 1, -2, -3, -4):
-        pl.semaphore_signal(barrier, inc=1, device_id=dev_at(by), device_id_type=MESH)
-    for by in range(1, nx):
-        pl.semaphore_signal(barrier, inc=1, device_id=x_at(by), device_id_type=MESH)
     for by in range(1, nz):
         @pl.when(mz + by < nz)
         def _():
@@ -112,7 +114,7 @@
     loads[1].wait()
     going = [None]
     for k in range(1, HOPS + 1):
-        target = lax.rem(me + k, n_dev)
+        target = dev_of(me + k)
         slot = jnp.int32(0)
         for j in range(SLOTS):
             slot = jnp.where(ddev[me * SLOTS + j] == target, j, slot)
@@ -161,10 +163,10 @@
     high_at = [jnp.int32(0)] * PATCHES
     low_at = []
     for beside in range(3):
-        place = lax.rem(me + beside - 1 + n_dev, n_dev)
+        place = dev_of(me + beside - 1)
         at = [jnp.int32(min(max(LOW_KEPT[beside] + q, 0), ENTRIES - 1)) for q in range(PATCHES)]
         for k in range(1, HOPS + 1):
-            source = lax.rem(place - k + n_dev, n_dev)
+            source = dev_of(place - k)
             landing = jnp.int32(-1)
             for j in range(SLOTS):
                 i = source * SLOTS + j
@@ -198,7 +200,7 @@
     column = iota((8, 4 * width), 1)
     target = jnp.zeros((8, 4 * width), jnp.int32)
     for i in range(nx):
-        source = mz * nx + lax.rem(mx - i + nx, nx)
+        source = (grp - mx) + ((mx - i) & (nx - 1))
         for q in range(PATCHES):
             at = (((column & (width - 1)) >> 3) == i) & ((column & 3) == q)
             target = jnp.where(at, cmap[0, source * PATCHES + q], target)
@@ -206,7 +208,7 @@
     same_half = (row8 >> 2) == ((iota((8, width), 1) >> 2) & 1)
     route = []
     for i in range(nz):
-        code = (lax.rem(mz + i, nz) * nx + mx) * PATCHES
+        code = (z_of(i) * nx + mx) * PATCHES
         route.append(jnp.where((target[:, :width] == code + (row8 & 3)) & same_half, 1.0, 0.0))
     route = jnp.concatenate(route, axis=0)
     wide_row, wide_column = iota((2 * nz, 4 * width), 0), iota((2 * nz, 4 * width), 1)
@@ -255,6 +257,25 @@
             send_sem=x_ss.at[i - 1], recv_sem=x_rs.at[i - 1], device_id=x_at(i), device_id_type=MESH)
         copy.start()
         x_copies.append(copy)
+
+    for copy in x_copies:
+        copy.wait_recv()
+    pool = jnp.concatenate([xpool[i * 16:i * 16 + 8, :] for i in range(nx)], axis=0)
+    routed = jnp.dot(route, pool, precision=HIGHEST, preferred_element_type=jnp.float32)
+    pool = jnp.concatenate([xpool[i * 16 + 8:i * 16 + 16, :] for i in range(nx)], axis=0)
+    group = iota((width, 128), 1) >> 5
+    pool = jnp.concatenate([jnp.where(group == t, pool, 0.0) for t in range(4)], axis=0)
+    routed_fifth = jnp.dot(wide_route, pool, precision=HIGHEST, preferred_element_type=jnp.float32)
+    for i in range(nz):
+        zbuf[i, 0:8, :] = routed[i * 8:i * 8 + 8]
+        zbuf[i, 8:10, :] = routed_fifth[i * 2:i * 2 + 2]
+    z_copies = []
+    for i in range(1, nz):
+        copy = pltpu.make_async_remote_copy(
+            src_ref=zbuf.at[i, pl.ds(0, 10)], dst_ref=zrecv.at[i - 1, pl.ds(0, 10)],
+            send_sem=z_ss.at[i - 1], recv_sem=z_rs.at[i - 1], device_id=z_at(i), device_id_type=MESH)
+        pl.when(mz + i >= nz)(copy.start)
+        z_copies.append((i, copy))
 
     ghost_copies = []
     for n, (by, first, to) in enumerate(((1, 1, 1), (-1, 0, 2 * PATCHES))):
@@ -276,25 +297,6 @@
         copy.start()
         inner_copies.append(copy)
 
-    for copy in x_copies:
-        copy.wait_recv()
-    pool = jnp.concatenate([xpool[i * 16:i * 16 + 8, :] for i in range(nx)], axis=0)
-    routed = jnp.dot(route, pool, precision=HIGHEST, preferred_element_type=jnp.float32)
-    pool = jnp.concatenate([xpool[i * 16 + 8:i * 16 + 16, :] for i in range(nx)], axis=0)
-    group = iota((width, 128), 1) >> 5
-    pool = jnp.concatenate([jnp.where(group == t, pool, 0.0) for t in range(4)], axis=0)
-    routed_fifth = jnp.dot(wide_route, pool, precision=HIGHEST, preferred_element_type=jnp.float32)
-    for i in range(nz):
-        zbuf[i, 0:8, :] = routed[i * 8:i * 8 + 8]
-        zbuf[i, 8:10, :] = routed_fifth[i * 2:i * 2 + 2]
-    z_copies = []
-    for i in sorted(range(1, nz), key=lambda i: -min(i, nz - i)):
-        copy = pltpu.make_async_remote_copy(
-            src_ref=zbuf.at[i, pl.ds(0, 10)], dst_ref=zrecv.at[i - 1, pl.ds(0, 10)],
-            send_sem=z_ss.at[i - 1], recv_sem=z_rs.at[i - 1], device_id=z_at(i), device_id_type=MESH)
-        pl.when(mz + i >= nz)(copy.start)
-        z_copies.append((i, copy))
-
     for copy in ghost_copies:
         copy.wait_recv()
     for q in range(PATCHES):
@@ -345,6 +347,19 @@
     for i in range(nz - 1):
         total = total + zrecv[i, 0:8, :]
         fifth = fifth + zrecv[i, 8:10, :]
+    sums[0:8, :] = total
+    sums[8:10, :] = fifth
+
+    for copy in edge_copies + ghost_copies + inner_copies + x_copies + z_copies:
+        copy.wait_send()
+
+
+def finish(adv, sums, adv_out, reg_out, reg_buf, adv_sem, reg_sem):
+    adv_copy = pltpu.make_async_copy(adv, adv_out, adv_sem)
+    adv_copy.start()
+    lane_in, lane_out = iota((128, 128), 0), iota((128, 128), 1)
+    lane8 = iota((8, 128), 1)
+    total, fifth = sums[0:8, :], sums[8:10, :]
     row = iota((8, 128), 0)
     fifth = jnp.where(row < 4, fifth[0:1], fifth[1:2])
     parts = [jnp.where(lane8 >> 5 == f, total, 0.0) for f in range(4)]
@@ -357,10 +372,11 @@
         block = wide[f * 8:f * 8 + 8]
         for half in range(2):
             chosen = jnp.where(inside & ((row & 3) >> 1 == half), block, 0.0)
-            reg[f, :, pl.ds(half * 128, 128)] = jnp.sum(chosen, axis=0, keepdims=True)
-
-    for copy in edge_copies + ghost_copies + inner_copies + x_copies + z_copies:
-        copy.wait_send()
+            reg_buf[f, :, pl.ds(half * 128, 128)] = jnp.sum(chosen, axis=0, keepdims=True)
+    reg_copy = pltpu.make_async_copy(reg_buf, reg_out, reg_sem)
+    reg_copy.start()
+    adv_copy.wait()
+    reg_copy.wait()
 
 
 def solution(mesh):
@@ -374,9 +390,9 @@
         hbm = pl.BlockSpec(memory_space=pltpu.HBM)
         f32 = jnp.float32
         dma = lambda n: pltpu.SemaphoreType.DMA((n,))
-        advanced, registers = pl.pallas_call(
+        advanced, sums = pl.pallas_call(
             functools.partial(kernel, nz, nx, n_dev),
-            out_shape=(pltpu.VMEM((640, 128), f32), pltpu.VMEM((FIELDS, 1, 256), f32)),
+            out_shape=(pltpu.VMEM((640, 128), f32), pltpu.VMEM((16, 128), f32)),
             in_specs=[hbm] * 5,
             out_specs=(vmem, vmem),
             scratch_shapes=[
@@ -396,6 +412,13 @@
             ],
             compiler_params=pltpu.CompilerParams(collective_id=0, has_side_effects=True, vmem_limit_bytes=24 * 1024 * 1024),
         )(*[pltpu.with_memory_space_constraint(a, pltpu.HBM) for a in (blocks, dest_dev, dest_slot, neighbours, coarse_map)])
+        advanced, registers = pl.pallas_call(
+            finish,
+            out_shape=(jax.ShapeDtypeStruct((640, 128), f32), jax.ShapeDtypeStruct((FIELDS, 1, 256), f32)),
+            in_specs=[pl.BlockSpec(memory_space=pl.ANY), vmem],
+            out_specs=(hbm, hbm),
+            scratch_shapes=[pltpu.VMEM((FIELDS, 1, 256), f32), pltpu.SemaphoreType.DMA, pltpu.SemaphoreType.DMA],
+        )(*[pltpu.with_memory_space_constraint(a, pltpu.VMEM) for a in (advanced, sums)])
         advanced = advanced.reshape(FIELDS, 32, PATCHES, 128).transpose(2, 0, 1, 3).reshape(PATCHES, FIELDS, 4096)
         return advanced, registers.transpose(1, 0, 2)
 

time: 32.1 us -> 31.3 us (0.975)
  local copies, waits for them, and re-layouts: 1.32 us -> 0 us
  Pallas kernels: 30 us -> 30.5 us
    unnamed x2 -> x0, local copies, waits for them, and re-layouts: 1.32 us -> none
    pallas_call x0 -> x1, Pallas kernels: none -> 0.81 us  [local(): pl.pallas_call(finish, out_shape=(jax.ShapeDtypeStruct((640, 128), f32),...]
    pallas_call x1, Pallas kernels: 30 us -> 29.7 us  [local(): pl.pallas_call(functools.partial(kernel, nz, nx, n_dev), out_shape=(pltpu...]
where the time goes in v5:
time: 31.3 us; the launch traced here: 31.1 us
  Pallas kernels  30.5 us (97%)
  between operations  0.64 us (2%)
    pallas_call x1, Pallas kernels, local(): pl.pallas_call(functools.partial(kernel, nz, nx, n_dev), out_shape=(pltpu...  29.7 us
    pallas_call x1, Pallas kernels, local(): pl.pallas_call(finish, out_shape=(jax.ShapeDtypeStruct((640, 128), f32),...  0.81 us

profile of v5, /device:TPU:24, one launch (start us, length us, event | category | flops | bytes accessed | tf_op | source)
XLA Modules:
  0.0 31.1 jit_solution(16387047899755695658)
XLA Ops:
  0.6 29.7 %shard_map.68 = (f32[640,128]{1,0:T(8,128)S(1)}, f32[16,128]{1,0:T(8,128)S(1)}) custom-call(f32[5,256,128]{2,1,0:T(8,128)} %bitcast.11, s32[128]{0:T(128)} %ddev_hbm.1, s32[128]{0:T(128)} %dslot_hbm.1, s32[2,64]{1,0:T(2,128)} %nbr_hbm.1, s32[1,192]{1,0:T(1,128)} %cmap_hbm.1), custom_call_target="tpu_custom_call" | custom-call | tf_op jit(solution)/shard_map/pallas_call | solution.py:393
  30.3 0.8 %shard_map.69 = (f32[640,128]{1,0:T(8,128)}, f32[5,1,256]{2,1,0:T(1,128)}) custom-call(f32[640,128]{1,0:T(8,128)S(1)} %get-tuple-element.6.adv, f32[16,128]{1,0:T(8,128)S(1)} %get-tuple-element.7.sums), custom_call_target="tpu_custom_call" | custom-call | tf_op jit(solution)/shard_map/pallas_call | solution.py:415

commit v6 on v5

--- a/solution.py
+++ b/solution.py
@@ -251,7 +251,7 @@
     xpool[0:8, :] = packed
     xpool[8:16, :] = coarse[32:40]
     x_copies = []
-    for i in range(1, nx):
+    for i in sorted(range(1, nx), key=lambda i: -min(i, nx - i)):
         copy = pltpu.make_async_remote_copy(
             src_ref=xpool.at[pl.ds(0, 16)], dst_ref=xpool.at[pl.ds(i * 16, 16)],
             send_sem=x_ss.at[i - 1], recv_sem=x_rs.at[i - 1], device_id=x_at(i), device_id_type=MESH)
@@ -396,16 +396,16 @@
             in_specs=[hbm] * 5,
             out_specs=(vmem, vmem),
             scratch_shapes=[
-                pltpu.VMEM((FIELDS, 32 * SLOTS, 128), f32), pltpu.SMEM(dest_dev.shape, jnp.int32), pltpu.SMEM(dest_slot.shape, jnp.int32),
+                pltpu.VMEM((FIELDS, 37 * SLOTS, 128), f32), pltpu.SMEM(dest_dev.shape, jnp.int32), pltpu.SMEM(dest_slot.shape, jnp.int32),
                 pltpu.SMEM(neighbours.shape, jnp.int32), pltpu.SMEM(coarse_map.shape, jnp.int32),
                 pltpu.SMEM((3 * PATCHES,), jnp.int32),
                 pltpu.VMEM((SLOTS, EDGE, 128), f32), pltpu.VMEM((SLOTS, EDGE, 128), f32),
                 pltpu.VMEM((SLOTS, INNER, 128), f32),
                 pltpu.VMEM((SENT, EDGE, 128), f32), pltpu.VMEM((ENTRIES, EDGE, 128), f32),
                 pltpu.VMEM((HOPS, INNER, 128), f32), pltpu.VMEM((HOPS, INNER, 128), f32),
-                pltpu.VMEM((3 * PATCHES, EDGE, 128), f32), pltpu.VMEM((80, 128), f32), pltpu.VMEM((80, 128), f32),
-                pltpu.VMEM((80, 128), f32), pltpu.VMEM((80, 128), f32),
-                pltpu.VMEM((480, 128), f32),
+                pltpu.VMEM((3 * PATCHES, EDGE, 128), f32), pltpu.VMEM((104, 128), f32), pltpu.VMEM((104, 128), f32),
+                pltpu.VMEM((104, 128), f32), pltpu.VMEM((104, 128), f32),
+                pltpu.VMEM((488, 128), f32),
                 pltpu.VMEM((nx * 16, 128), f32), pltpu.VMEM((nz, 16, 128), f32), pltpu.VMEM((max(nz - 1, 1), 16, 128), f32),
                 dma(len(AHEAD)), dma(len(AHEAD)), dma(HOPS), dma(HOPS), dma(2), dma(2),
                 dma(max(nx - 1, 1)), dma(max(nx - 1, 1)), dma(max(nz - 1, 1)), dma(max(nz - 1, 1)), dma(7), pltpu.SemaphoreType.REGULAR,

time: 31.3 us -> 31.2 us (level)
  no operation moved by 1% of the time
where the time goes in v6:
time: 31.2 us; the launch traced here: 31 us
  Pallas kernels  30.4 us (97%)
  between operations  0.64 us (2%)
    pallas_call x1, Pallas kernels, local(): pl.pallas_call(functools.partial(kernel, nz, nx, n_dev), out_shape=(pltpu...  29.6 us
    pallas_call x1, Pallas kernels, local(): pl.pallas_call(finish, out_shape=(jax.ShapeDtypeStruct((640, 128), f32),...  0.81 us

profile of v6, /device:TPU:24, one launch (start us, length us, event | category | flops | bytes accessed | tf_op | source)
XLA Modules:
  0.0 31.0 jit_solution(6409540684146224498)
XLA Ops:
  0.6 29.6 %shard_map.68 = (f32[640,128]{1,0:T(8,128)S(1)}, f32[16,128]{1,0:T(8,128)S(1)}) custom-call(f32[5,256,128]{2,1,0:T(8,128)} %bitcast.11, s32[128]{0:T(128)} %ddev_hbm.1, s32[128]{0:T(128)} %dslot_hbm.1, s32[2,64]{1,0:T(2,128)} %nbr_hbm.1, s32[1,192]{1,0:T(1,128)} %cmap_hbm.1), custom_call_target="tpu_custom_call" | custom-call | tf_op jit(solution)/shard_map/pallas_call | solution.py:393
  30.2 0.8 %shard_map.69 = (f32[640,128]{1,0:T(8,128)}, f32[5,1,256]{2,1,0:T(1,128)}) custom-call(f32[640,128]{1,0:T(8,128)S(1)} %get-tuple-element.6.adv, f32[16,128]{1,0:T(8,128)S(1)} %get-tuple-element.7.sums), custom_call_target="tpu_custom_call" | custom-call | tf_op jit(solution)/shard_map/pallas_call | solution.py:415

commit v7 on v6

--- a/solution.py
+++ b/solution.py
@@ -21,11 +21,11 @@
 INNER = 120
 
 AHEAD = (
+    (-1, 14, (("kept", 0), ("kept", 1), ("kept", 2))),
     (4, 13, (("low", 3),)),
     (3, 10, (("low", 2), ("low", 3), ("high", 3))),
     (2, 6, (("low", 1), ("low", 2), ("low", 3), ("high", 2))),
     (1, 0, (("kept", 1), ("kept", 2), ("kept", 3), ("low", 1), ("low", 2), ("high", 1))),
-    (-1, 14, (("kept", 0), ("kept", 1), ("kept", 2))),
 )
 SENT = 17
 OWN = SENT

time: 31.2 us -> 31.2 us (level)
  no operation moved by 1% of the time
where the time goes in v7:
time: 31.2 us; the launch traced here: 31 us
  Pallas kernels  30.4 us (97%)
  between operations  0.64 us (2%)
    pallas_call x1, Pallas kernels, local(): pl.pallas_call(functools.partial(kernel, nz, nx, n_dev), out_shape=(pltpu...  29.6 us
    pallas_call x1, Pallas kernels, local(): pl.pallas_call(finish, out_shape=(jax.ShapeDtypeStruct((640, 128), f32),...  0.81 us

profile of v7, /device:TPU:24, one launch (start us, length us, event | category | flops | bytes accessed | tf_op | source)
XLA Modules:
  0.0 31.0 jit_solution(13588103912061823505)
XLA Ops:
  0.6 29.6 %shard_map.68 = (f32[640,128]{1,0:T(8,128)S(1)}, f32[16,128]{1,0:T(8,128)S(1)}) custom-call(f32[5,256,128]{2,1,0:T(8,128)} %bitcast.11, s32[128]{0:T(128)} %ddev_hbm.1, s32[128]{0:T(128)} %dslot_hbm.1, s32[2,64]{1,0:T(2,128)} %nbr_hbm.1, s32[1,192]{1,0:T(1,128)} %cmap_hbm.1), custom_call_target="tpu_custom_call" | custom-call | tf_op jit(solution)/shard_map/pallas_call | solution.py:393
  30.2 0.8 %shard_map.69 = (f32[640,128]{1,0:T(8,128)}, f32[5,1,256]{2,1,0:T(1,128)}) custom-call(f32[640,128]{1,0:T(8,128)S(1)} %get-tuple-element.6.adv, f32[16,128]{1,0:T(8,128)S(1)} %get-tuple-element.7.sums), custom_call_target="tpu_custom_call" | custom-call | tf_op jit(solution)/shard_map/pallas_call | solution.py:415
